TPU v7x, 32 devices: a whole 2x2x4 slice. The times are simulated.
32 devices in a mesh: rep: 2 (over y), seq: 4 (over z), head: 4 (over x, core).
Axes of the slice: x: 2, y: 2, z: 4, core: 2. Of those that a mesh axis runs over, the one named last changes fastest.
Arguments:
- queries: bfloat16 [4096, 1024], P(('rep', 'seq', 'head')), parts along dimension 0, may hold values from -6 to 6
- keys: bfloat16 [4096, 2, 1024], P(('rep', 'seq', 'head')), parts along dimension 0, may hold values from -6 to 6
- values: bfloat16 [4096, 2, 1024], P(('rep', 'seq', 'head')), parts along dimension 0, may hold values from -6 to 6
- out_gate: bfloat16 [4096, 1024], P(('rep', 'seq', 'head')), parts along dimension 0, may hold values from -6 to 6
- write_rate: bfloat16 [4096, 2, 8], P(('rep', 'seq', 'head')), parts along dimension 0, may hold values from 0 to 2
- log_decay: bfloat16 [4096, 8], P(('rep', 'seq', 'head')), parts along dimension 0, may hold values from -0.7 to 0
- doc_starts: int32 [8], P('rep'), parts along dimension 0, may hold values from 0 to 2047, as said below
- norm_gain: float32 [128], replicated, may hold values from 0.1 to 1.9
- out_weight: bfloat16 [1024, 2048], P(None, 'head'), may hold values from -0.1875 to 0.1875
Outputs:
- layer_out: bfloat16 [4096, 2048], P(('rep', 'seq'), 'head'), parts along dimension 0
There are 2 independent parts, one for each index of `rep`. A program takes and returns all parts, laid end to end along the dimension named above; an argument that names none is the same for every part. Nothing has to cross between parts.
Inputs may be any that keep to these rules, and one draw needn't show every extreme that they name: `doc_starts`: rises strictly from 0; one document holds exactly 1024 tokens, every other fewer, each at least one.
All inputs are finite; a program needn't handle non-finite values.
Results may differ from a plain program's by a relative error of at most 0.007.
Values may be sent and summed in bfloat16 or wider, within the bound.
A program may use at most 64 MiB of HBM per device.

v0:
```python
import math

import jax
import jax.numpy as jnp
from jax import lax
from jax.sharding import PartitionSpec as P

PRECISE_SETTING = lax.Precision.HIGHEST


def passed_along(value, axis, steps):
    count = lax.axis_size(axis)
    initial, last = (max(0, -steps), min(count, count - steps))
    return lax.ppermute(value, axis, [(source, source + steps) for source in range(initial, last)])


def doc_index(token_position, doc_starts):
    return jnp.sum((token_position[:, None] >= doc_starts[None, :]).astype(jnp.int32), 1) - 1


def advance(carry_pair, step_pair):
    current_state, through_map = carry_pair
    step_map, step_add = step_pair
    new_state = (
        jnp.einsum("hde,hef->hdf", step_map, current_state, precision=PRECISE_SETTING) + step_add
    )
    new_map = jnp.einsum("hde,hef->hdf", step_map, through_map, precision=PRECISE_SETTING)
    return ((new_state, new_map), (current_state, through_map))


def stretch_pieces(
    query_part,
    key_part,
    value_part,
    rate_part,
    decay_part,
    first_pos,
    doc_starts,
    heads_here,
    head_depth,
):
    group_len = query_part.shape[0]
    steps_len = 2 * group_len
    block_len = math.gcd(128, steps_len)
    block_count = steps_len // block_len
    half_len = block_len // 2
    read_rows = (
        query_part.reshape(group_len, heads_here, head_depth).astype(jnp.float32).transpose(1, 0, 2)
    )
    read_rows = read_rows.reshape(heads_here, block_count, half_len, head_depth)
    key_rows = key_part.reshape(group_len, 2, heads_here, head_depth).astype(jnp.float32)
    key_rows = key_rows / jnp.sqrt(jnp.sum(key_rows * key_rows, -1, keepdims=True) + 1e-06)
    key_rows = key_rows.transpose(2, 0, 1, 3).reshape(
        heads_here, block_count, block_len, head_depth
    )
    value_rows = value_part.reshape(group_len, 2, heads_here, head_depth).astype(jnp.float32)
    value_rows = value_rows.transpose(2, 0, 1, 3).reshape(
        heads_here, block_count, block_len, head_depth
    )
    rate_rows = (
        rate_part.astype(jnp.float32).transpose(2, 0, 1).reshape(heads_here, block_count, block_len)
    )
    decay_logs = decay_part.reshape(group_len, heads_here).astype(jnp.float32)
    decay_logs = jnp.stack([decay_logs, jnp.zeros_like(decay_logs)], 1).transpose(2, 0, 1)
    totals = jnp.cumsum(decay_logs.reshape(heads_here, block_count, block_len), -1)
    doc_ids = doc_index(first_pos + jnp.arange(group_len, dtype=jnp.int32), doc_starts)
    doc_before = doc_index(jnp.reshape(first_pos - 1, (1,)), doc_starts)
    step_docs = jnp.repeat(doc_ids, 2).reshape(block_count, block_len)
    prior_docs = jnp.concatenate([doc_before, step_docs[:-1, -1]])
    step_index = jnp.arange(block_len)
    within = step_index[:, None] >= step_index[None, :]
    strict = step_index[:, None] > step_index[None, :]
    same_doc = step_docs[:, :, None] == step_docs[:, None, :]
    causal_doc = within & same_doc
    spread = totals[..., :, None] - totals[..., None, :]
    decay_ratio = jnp.where(causal_doc, jnp.exp(jnp.where(causal_doc, spread, 0.0)), 0.0)
    start_gain = jnp.where(step_docs == prior_docs[:, None], jnp.exp(totals), 0.0)
    end_gain = jnp.where(step_docs == step_docs[:, -1:], jnp.exp(totals[..., -1:] - totals), 0.0)
    key_gram = jnp.einsum("hcid,hcjd->hcij", key_rows, key_rows, precision=PRECISE_SETTING)
    lower_part = jnp.where(strict, rate_rows[..., :, None] * decay_ratio * key_gram, 0.0)
    system = lower_part + jnp.eye(block_len, dtype=jnp.float32)
    right_side = jnp.concatenate(
        [rate_rows[..., None] * value_rows, (rate_rows * start_gain)[..., None] * key_rows], -1
    )
    solved = jax.scipy.linalg.solve_triangular(system, right_side, lower=True, unit_diagonal=True)
    written = solved[..., :head_depth]
    erased = solved[..., head_depth:]
    scores = (
        jnp.einsum("hcrd,hcjd->hcrj", read_rows, key_rows, precision=PRECISE_SETTING)
        * decay_ratio[:, :, 1::2, :]
    )
    inner_out = jnp.einsum("hcrj,hcje->hcre", scores, written, precision=PRECISE_SETTING)
    carried = start_gain[:, :, 1::2, None] * read_rows - jnp.einsum(
        "hcrj,hcje->hcre", scores, erased, precision=PRECISE_SETTING
    )
    weighted = end_gain[..., None] * key_rows
    identity_map = jnp.broadcast_to(
        jnp.eye(head_depth, dtype=jnp.float32), (heads_here, head_depth, head_depth)
    )
    transition = start_gain[..., -1, None, None] * identity_map[:, None] - jnp.einsum(
        "hcid,hcie->hcde", weighted, erased, precision=PRECISE_SETTING
    )
    fresh_state = jnp.einsum("hcid,hcie->hcde", weighted, written, precision=PRECISE_SETTING)
    zero_state = jnp.zeros((heads_here, head_depth, head_depth), jnp.float32)
    ends_pair, starts_pair = lax.scan(
        advance,
        (zero_state, identity_map),
        (transition.transpose(1, 0, 2, 3), fresh_state.transpose(1, 0, 2, 3)),
    )
    local_end, local_map = ends_pair
    block_starts, block_maps = starts_pair
    return (inner_out, carried, block_starts, block_maps, local_end, local_map)


def finish_readout(inner_out, carried, block_starts, block_maps, incoming):
    heads_here = inner_out.shape[0]
    head_depth = inner_out.shape[-1]
    begin_state = block_starts + jnp.einsum(
        "chde,hef->chdf", block_maps, incoming, precision=PRECISE_SETTING
    )
    readout = inner_out + jnp.einsum(
        "hcrd,chde->hcre", carried, begin_state, precision=PRECISE_SETTING
    )
    return readout.reshape(heads_here, -1, head_depth).transpose(1, 0, 2)


def norm_rows(readout, gate_part, norm_gain):
    group_len, heads_here, head_depth = readout.shape
    gate_vals = gate_part.reshape(group_len, heads_here, head_depth).astype(jnp.float32)
    inv_rms = lax.rsqrt(jnp.mean(readout * readout, -1, keepdims=True) + 1e-05)
    normed = (readout * inv_rms * norm_gain * jax.nn.silu(gate_vals)).astype(jnp.bfloat16)
    return normed.reshape(group_len, heads_here * head_depth)


def chain_states(local_map, local_end):
    heads_here, head_depth = (local_map.shape[0], local_map.shape[1])
    zero_state = jnp.zeros((heads_here, head_depth, head_depth), jnp.float32)

    def relay_once(turn_index, incoming):
        outgoing = (
            jnp.einsum("hde,hef->hdf", local_map, incoming, precision=PRECISE_SETTING) + local_end
        )
        return passed_along(outgoing.astype(jnp.bfloat16), "seq", 1).astype(outgoing.dtype)

    incoming = lax.fori_loop(0, lax.axis_size("seq") - 1, relay_once, zero_state)
    return incoming


def on_device(
    queries, keys, values, out_gate, write_rate, log_decay, doc_starts, norm_gain, out_weight
):
    tok_dev, feature_width = queries.shape
    heads_all = log_decay.shape[1]
    groups = lax.axis_size("head")
    local_heads = heads_all // groups
    head_depth = feature_width // heads_all
    arrived = (
        lax.all_to_all(queries[:, None, :], "head", split_axis=2, concat_axis=0, tiled=True),
        lax.all_to_all(keys, "head", split_axis=2, concat_axis=0, tiled=True),
        lax.all_to_all(values, "head", split_axis=2, concat_axis=0, tiled=True),
        lax.all_to_all(out_gate[:, None, :], "head", split_axis=2, concat_axis=0, tiled=True),
        lax.all_to_all(write_rate, "head", split_axis=2, concat_axis=0, tiled=True),
        lax.all_to_all(log_decay[:, None, :], "head", split_axis=2, concat_axis=0, tiled=True),
    )
    query_part, key_part, value_part, gate_part, rate_part, decay_part = arrived
    group_len = query_part.shape[0]
    first_pos = lax.axis_index("seq") * group_len
    inner_out, carried, block_starts, block_maps, local_end, local_map = stretch_pieces(
        query_part,
        key_part,
        value_part,
        rate_part,
        decay_part,
        first_pos,
        doc_starts,
        local_heads,
        head_depth,
    )
    incoming = chain_states(local_map, local_end)
    readout = finish_readout(inner_out, carried, block_starts, block_maps, incoming)
    normed = norm_rows(readout, gate_part, norm_gain)
    acc_total = jnp.dot(
        lax.all_gather(normed, "head", axis=1, tiled=True),
        out_weight,
        preferred_element_type=jnp.float32,
    )
    return acc_total.astype(jnp.bfloat16)


def solution(mesh):
    placed = (
        P(("rep", "seq", "head"), None),
        P(("rep", "seq", "head"), None, None),
        P(("rep", "seq", "head"), None, None),
        P(("rep", "seq", "head"), None),
        P(("rep", "seq", "head"), None, None),
        P(("rep", "seq", "head"), None),
        P("rep"),
        P(),
        P(None, "head"),
    )
    return jax.shard_map(
        on_device, mesh=mesh, in_specs=placed, out_specs=P(("rep", "seq"), "head"), check_vma=False
    )
```

profile of v0, /device:TPU:25, one launch (start us, length us, event | category | flops | bytes accessed | tf_op | source)
XLA Modules:
  0.0 341.2 jit_solution(240848373415669369)
XLA Ops:
  6.5 0.8 copy.215
  8.0 3.9 %all-to-all-start.2 = ((bf16[4,2,128]{2,1,0:T(2,128)(2,1)}), bf16[4,2,128]{2,1,0:T(2,128)(2,1)S(1)}, u32[]{:S(2)}, u32[]{:S(2)}) async-start(bf16[4,2,128]{2,1,0:T(2,128)(2,1)} %bitcast.133), calls=%async_computation.2 | async-start | bytes 4096 | tf_op jit(solution)/shard_map/all_to_all | solution.py:163
  11.9 0.7 convert_reduce_fusion
  12.9 0.7 fusion.44
  13.6 1.3 fusion.46
  15.5 0.7 iota_compare_fusion.2
  16.6 1.3 copy.175
  19.2 1.3 copy.167
  21.0 2.2 reduce.6
  23.2 0.8 reshape.194
  24.0 1.9 copy.164
  25.9 1.9 copy.177
  28.1 2.2 reduce.7
  30.3 0.8 reshape.196
  31.1 3.3 all-to-all-start.3
  35.5 2.0 all-to-all-done.3
  37.5 4.1 %all-to-all-start.1 = ((bf16[4,2,16384]{2,1,0:T(2,128)(2,1)}), bf16[4,2,16384]{2,1,0:T(2,128)(2,1)S(1)}, u32[]{:S(2)}, u32[]{:S(2)}) async-start(bf16[4,2,16384]{2,1,0:T(2,128)(2,1)} %reshape.194), calls=%async_computation.1 | async-start | bytes 524288 | tf_op jit(solution)/shard_map/all_to_all | solution.py:158
  41.9 1.5 slice.30
  43.5 3.2 all-to-all-done.1
  46.7 4.2 %all-to-all-start.5 = ((bf16[4,2,16384]{2,1,0:T(2,128)(2,1)}), bf16[4,2,16384]{2,1,0:T(2,128)(2,1)S(1)}, u32[]{:S(2)}, u32[]{:S(2)}) async-start(bf16[4,2,16384]{2,1,0:T(2,128)(2,1)} %reshape.196), calls=%async_computation.5 | async-start | bytes 524288 | tf_op jit(solution)/shard_map/all_to_all | solution.py:161
  51.5 4.7 %all-to-all-done.5 = bf16[4,2,16384]{2,1,0:T(2,128)(2,1)S(1)} async-done(((bf16[4,2,16384]{2,1,0:T(2,128)(2,1)}), bf16[4,2,16384]{2,1,0:T(2,128)(2,1)S(1)}, u32[]{:S(2)}, u32[]{:S(2)}) %all-to-all-start.5) | async-done | bytes 262176 | tf_op jit(solution)/shard_map/all_to_all | solution.py:161
  56.1 4.3 %all-to-all-start = ((bf16[128,2,1024]{0,1,2:T(2,128)(2,1)}), bf16[128,2,1024]{0,1,2:T(2,128)(2,1)S(1)}, u32[]{:S(2)}, u32[]{:S(2)}) async-start(bf16[128,2,1024]{0,1,2:T(2,128)(2,1)} %copy.164), calls=%async_computation | async-start | bytes 1048576 | tf_op jit(solution)/shard_map/all_to_all | solution.py:159
  61.1 0.8 slice.33
  61.9 0.7 slice_reduce_fusion.1
  63.1 0.7 copy.169
  64.9 1.1 reshape.175
  66.0 2.5 all-to-all-done
  68.4 5.0 %all-to-all-start.4 = ((bf16[128,2,1024]{0,1,2:T(2,128)(2,1)}), bf16[128,2,1024]{0,1,2:T(2,128)(2,1)}, u32[]{:S(2)}, u32[]{:S(2)}) async-start(bf16[128,2,1024]{0,1,2:T(2,128)(2,1)} %copy.177), calls=%async_computation.4 | async-start | bytes 1048576 | tf_op jit(solution)/shard_map/all_to_all | solution.py:160
  74.4 1.2 multiply_reduce_fusion
  75.7 1.4 divide_bitcast_fusion
  77.1 0.8 copy.166
  77.9 3.6 %all-to-all-done.4 = bf16[128,2,1024]{0,1,2:T(2,128)(2,1)} async-done(((bf16[128,2,1024]{0,1,2:T(2,128)(2,1)}), bf16[128,2,1024]{0,1,2:T(2,128)(2,1)}, u32[]{:S(2)}, u32[]{:S(2)}) %all-to-all-start.4) | async-done | bytes 524320 | tf_op jit(solution)/shard_map/all_to_all | solution.py:160
  81.5 1.4 copy.178
  82.9 1.5 reshape.181
  84.4 3.0 copy.179
  87.5 3.4 %fusion.26 = f32[2,8,1,128,128]{4,3,2,1,0:T(8,128)} fusion(f32[2,8,128,128]{3,2,1,0:T(8,128)S(1)} %bitcast.148, f32[128,128]{1,0:T(8,128)S(1)} %copy-done.16, f32[128,128]{1,0:T(8,128)S(1)} %copy-done.7, f32[2,8,128]{2,1,0:T(8,128)S(1)} %copy-done.15, pred[128,128]{1,0:T(8,128)(4,1)S(1)} %copy-done.19, pred[128,128]{1,0:T(8,128)(4,1)S(1)} %copy-done.20, ...), kind=kOutput, calls=%fused_computation.35 | convolution fusion | flops 405012480 | bytes 2408448 | tf_op jit(solution)/shard_map/hcid,hcjd->hcij/dot_general | solution.py:79
  91.0 158.6 %custom-call.4 = f32[2,8,1,128,128]{3,4,2,1,0:T(8,128)} custom-call(f32[2,8,1,128,128]{4,3,2,1,0:T(8,128)} %fusion.26), custom_call_target="InvertDiagBlocksLowerTriangular" | custom-call | tf_op jit(solution)/shard_map/jit(_solve_triangular)/vmap(vmap())/triangular_solve | solution.py:85
  249.6 2.3 fusion.27
  253.2 2.0 fusion.16
  255.2 1.9 fusion.33
  257.1 1.9 convolution_subtract_fusion
  259.0 3.2 convolution_bitcast_fusion.1
  262.2 2.2 fusion.21
  264.5 23.6 %while.28 = (s32[]{:T(128)}, f32[2,128,128]{2,1,0:T(8,128)S(1)}, f32[2,128,128]{2,1,0:T(8,128)S(1)}, f32[8,2,128,128]{2,3,1,0:T(8,128)}, f32[8,2,128,128]{3,2,1,...) while((s32[]{:T(128)}, f32[2,128,128]{2,1,0:T(8,128)S(1)}, ...), condition=%wide.region_5.6_spmd.clone, body=%wide.region_4.5_spmd.clone.sunk | while | flops 100761600 | bytes 2492027 | solution.py:105
  264.6 1.2 convolution_add_fusion.4
  267.5 1.2 convolution_add_fusion.4
  270.5 1.2 convolution_add_fusion.4
  273.4 1.2 convolution_add_fusion.4
  276.4 1.2 convolution_add_fusion.4
  279.3 1.2 convolution_add_fusion.4
  282.3 1.2 convolution_add_fusion.4
  285.3 1.2 convolution_add_fusion.4
  288.1 16.2 %while.29 = (s32[]{:T(128)}, f32[2,128,128]{2,1,0:T(8,128)S(1)}, f32[2,128,128]{2,1,0:T(8,128)S(1)}, f32[2,128,128]{2,1,0:T(8,128)S(1)}, s32[]{:T(128)}, /*index=5*/s32[]{:T(128)}) while((s32[]{:T(128)}, f32[2,128,128]{2,1,0:T(8,128)S(1)}, f32[2,128,128]{2,1,0:T(8,128)S(1)}, f32[2,128,128]{2,1,0:T(8,128)S(1)}, s32[]{:T(128)}, ...), condition=%wide.region_7.8_spmd.clone, body=%wide.region_6.7_spmd.clone.sunk | while | flops 50462720 | bytes 917623 | solution.py:145
  288.4 1.3 collective-permute-start
  289.7 3.7 %collective-permute-done = bf16[2,128,128]{2,1,0:T(8,128)(2,1)S(1)} collective-permute-done((bf16[2,128,128]{2,1,0:T(8,128)(2,1)S(1)}, bf16[2,128,128]{2,1,0:T(8,128)(2,1)S(1)}, u32[]{:S(2)}, u32[]{:S(2)}) %collective-permute-start) | collective-permute-done | bytes 65568 | tf_op jit(solution)/shard_map/while/body/eval_jaxpr/ppermute | solution.py:14
  293.8 1.3 collective-permute-start
  295.1 3.7 %collective-permute-done = bf16[2,128,128]{2,1,0:T(8,128)(2,1)S(1)} collective-permute-done((bf16[2,128,128]{2,1,0:T(8,128)(2,1)S(1)}, bf16[2,128,128]{2,1,0:T(8,128)(2,1)S(1)}, u32[]{:S(2)}, u32[]{:S(2)}) %collective-permute-start) | collective-permute-done | bytes 65568 | tf_op jit(solution)/shard_map/while/body/eval_jaxpr/ppermute | solution.py:14
  299.1 1.3 collective-permute-start
  300.4 3.7 %collective-permute-done = bf16[2,128,128]{2,1,0:T(8,128)(2,1)S(1)} collective-permute-done((bf16[2,128,128]{2,1,0:T(8,128)(2,1)S(1)}, bf16[2,128,128]{2,1,0:T(8,128)(2,1)S(1)}, u32[]{:S(2)}, u32[]{:S(2)}) %collective-permute-start) | collective-permute-done | bytes 65568 | tf_op jit(solution)/shard_map/while/body/eval_jaxpr/ppermute | solution.py:14
  304.4 2.7 fusion.20
  307.1 2.1 convolution_add_fusion.2
  309.7 0.9 copy.194
  310.6 21.0 %all-gather.2.cloned.1.call-done = bf16[512,1024]{0,1:T(8,128)(2,1)} async-done(((bf16[512,256]{0,1:T(8,128)(2,1)}), bf16[512,1024]{0,1:T(8,128)(2,1)}) %all-gather.2.cloned.1.call-update) | async-done | bytes 1048592 | tf_op jit(solution)/shard_map/all_gather | solution.py:183
  331.6 2.8 convolution_convert_fusion
  (164 shorter events, 25.0 us)
Async XLA Ops:
  6.5 325.1 %copy-start = (bf16[1024,512]{1,0:T(8,128)(2,1)S(1)}, bf16[1024,512]{1,0:T(8,128)(2,1)}, u32[]{:S(2)}) copy-start(bf16[1024,512]{1,0:T(8,128)(2,1)} %param.21) | copy-start | bytes 3145732
  6.5 17.4 %copy-start.11 = (bf16[128,2,1024]{2,1,0:T(2,128)(2,1)S(1)}, bf16[128,2,1024]{2,1,0:T(2,128)(2,1)}, u32[]{:S(2)}) copy-start(bf16[128,2,1024]{2,1,0:T(2,128)(2,1)} %param.14) | copy-start | bytes 1572868
  6.5 19.3 %copy-start.12 = (bf16[128,2,1024]{2,1,0:T(2,128)(2,1)S(1)}, bf16[128,2,1024]{2,1,0:T(2,128)(2,1)}, u32[]{:S(2)}) copy-start(bf16[128,2,1024]{2,1,0:T(2,128)(2,1)} %param.15) | copy-start | bytes 1572868
  8.0 23.1 %all-to-all-start.2 = ((bf16[4,2,128]{2,1,0:T(2,128)(2,1)}), bf16[4,2,128]{2,1,0:T(2,128)(2,1)S(1)}, u32[]{:S(2)}, u32[]{:S(2)}) async-start(bf16[4,2,128]{2,1,0:T(2,128)(2,1)} %bitcast.133), calls=%async_computation.2 | async-start | bytes 4096 | tf_op jit(solution)/shard_map/all_to_all | solution.py:163
  16.5 25.0 %copy-start.9 = (pred[8,128,128]{2,1,0:T(8,128)(4,1)}, pred[8,128,128]{2,1,0:T(8,128)(4,1)S(1)}, u32[]{:S(2)}) copy-start(pred[8,128,128]{2,1,0:T(8,128)(4,1)S(1)} %compare_and_fusion) | copy-start | bytes 393220
  19.2 8.6 %copy-start.13 = (bf16[128,1024]{1,0:T(8,128)(2,1)S(1)}, bf16[128,1024]{1,0:T(8,128)(2,1)}, u32[]{:S(2)}) copy-start(bf16[128,1024]{1,0:T(8,128)(2,1)} %param.16) | copy-start | bytes 786436
  31.1 6.4 %all-to-all-start.3 = ((bf16[128,2,8]{0,1,2:T(2,128)(2,1)}), bf16[128,2,8]{0,1,2:T(2,128)(2,1)S(1)}, u32[]{:S(2)}, u32[]{:S(2)}) async-start(bf16[128,2,8]{0,1,2:T(2,128)(2,1)} %copy.175), calls=%async_computation.3 | async-start | bytes 8192 | tf_op jit(solution)/shard_map/all_to_all | solution.py:162
  37.5 9.2 %all-to-all-start.1 = ((bf16[4,2,16384]{2,1,0:T(2,128)(2,1)}), bf16[4,2,16384]{2,1,0:T(2,128)(2,1)S(1)}, u32[]{:S(2)}, u32[]{:S(2)}) async-start(bf16[4,2,16384]{2,1,0:T(2,128)(2,1)} %reshape.194), calls=%async_computation.1 | async-start | bytes 524288 | tf_op jit(solution)/shard_map/all_to_all | solution.py:158
  41.9 18.5 %copy-start.22 = (pred[8,128]{1,0:T(8,128)(4,1)S(1)}, pred[8,128]{1,0:T(8,128)(4,1)}, u32[]{:S(2)}) copy-start(pred[8,128]{1,0:T(8,128)(4,1)} %copy.182) | copy-start | bytes 3076
  41.9 18.5 %copy-start.23 = (pred[8,128]{1,0:T(8,128)(4,1)S(1)}, pred[8,128]{1,0:T(8,128)(4,1)}, u32[]{:S(2)}) copy-start(pred[8,128]{1,0:T(8,128)(4,1)} %copy.180) | copy-start | bytes 3076
  46.7 9.4 %all-to-all-start.5 = ((bf16[4,2,16384]{2,1,0:T(2,128)(2,1)}), bf16[4,2,16384]{2,1,0:T(2,128)(2,1)S(1)}, u32[]{:S(2)}, u32[]{:S(2)}) async-start(bf16[4,2,16384]{2,1,0:T(2,128)(2,1)} %reshape.196), calls=%async_computation.5 | async-start | bytes 524288 | tf_op jit(solution)/shard_map/all_to_all | solution.py:161
  51.5 11.4 %copy-start.14 = (f32[2,8,128]{2,1,0:T(8,128)}, f32[2,8,128]{2,1,0:T(8,128)S(1)}, u32[]{:S(2)}) copy-start(f32[2,8,128]{2,1,0:T(8,128)S(1)} %reshape.172) | copy-start | bytes 24580
  56.1 12.3 %all-to-all-start = ((bf16[128,2,1024]{0,1,2:T(2,128)(2,1)}), bf16[128,2,1024]{0,1,2:T(2,128)(2,1)S(1)}, u32[]{:S(2)}, u32[]{:S(2)}) async-start(bf16[128,2,1024]{0,1,2:T(2,128)(2,1)} %copy.164), calls=%async_computation | async-start | bytes 1048576 | tf_op jit(solution)/shard_map/all_to_all | solution.py:159
  68.4 13.1 %all-to-all-start.4 = ((bf16[128,2,1024]{0,1,2:T(2,128)(2,1)}), bf16[128,2,1024]{0,1,2:T(2,128)(2,1)}, u32[]{:S(2)}, u32[]{:S(2)}) async-start(bf16[128,2,1024]{0,1,2:T(2,128)(2,1)} %copy.177), calls=%async_computation.4 | async-start | bytes 1048576 | tf_op jit(solution)/shard_map/all_to_all | solution.py:160
  73.4 258.2 %all-gather.2.cloned.1.call-start = ((), (), s32[]{:S(2)}) async-start(), calls=%async_computation.6 | async-start | bytes 1310720 | tf_op jit(solution)/shard_map/all_gather | solution.py:183
  82.9 4.6 %copy-start.7 = (f32[128,128]{1,0:T(8,128)S(1)}, f32[128,128]{1,0:T(8,128)}, u32[]{:S(2)}) copy-start(f32[128,128]{1,0:T(8,128)} %get-tuple-element.189) | copy-start | bytes 196612
  82.9 4.6 %copy-start.15 = (f32[2,8,128]{2,1,0:T(8,128)S(1)}, f32[2,8,128]{2,1,0:T(8,128)}, u32[]{:S(2)}) copy-start(f32[2,8,128]{2,1,0:T(8,128)} %copy-done.14) | copy-start | bytes 24580
  82.9 4.6 %copy-start.19 = (pred[128,128]{1,0:T(8,128)(4,1)S(1)}, pred[128,128]{1,0:T(8,128)(4,1)}, u32[]{:S(2)}) copy-start(pred[128,128]{1,0:T(8,128)(4,1)} %get-tuple-element.187) | copy-start | bytes 49156
  82.9 4.6 %copy-start.20 = (pred[128,128]{1,0:T(8,128)(4,1)S(1)}, pred[128,128]{1,0:T(8,128)(4,1)}, u32[]{:S(2)}) copy-start(pred[128,128]{1,0:T(8,128)(4,1)} %get-tuple-element.188) | copy-start | bytes 49156
  84.4 3.1 copy-start.10
  84.4 3.1 copy-start.16
  87.5 162.1 %copy-start.2 = (bf16[2,512,128]{2,1,0:T(8,128)(2,1)S(1)}, bf16[2,512,128]{2,1,0:T(8,128)(2,1)}, u32[]{:S(2)}) copy-start(bf16[2,512,128]{2,1,0:T(8,128)(2,1)} %copy.169) | copy-start | bytes 786436
  91.0 161.0 %copy-start.18 = (f32[2,8,128]{2,1,0:T(8,128)S(1)}, f32[2,8,128]{2,1,0:T(8,128)}, u32[]{:S(2)}) copy-start(f32[2,8,128]{2,1,0:T(8,128)} %get-tuple-element.182) | copy-start | bytes 24580
  249.6 2.3 copy-start.1
  252.0 1.2 copy-start.6
  255.2 1.9 copy-start.17
  259.0 3.2 copy-start.8
  259.0 3.2 copy-start.21
  288.4 5.0 %collective-permute-start = (bf16[2,128,128]{2,1,0:T(8,128)(2,1)S(1)}, bf16[2,128,128]{2,1,0:T(8,128)(2,1)S(1)}, u32[]{:S(2)}, u32[]{:S(2)}) collective-permute-start(bf16[2,128,128]{2,1,0:T(8,128)(2,1)S(1)} %fusion.76), channel_id=1, source_target_pairs={{0,4},{4,8},{8,12},{1,5},{5,9},{9,13},{2,6},{6,10},{10,14},{3,7},{... | collective-permute-start | bytes 196616 | tf_op jit(solution)/shard_map/while/body/eval_jaxpr/ppermute | solution.py:14
  293.8 5.0 %collective-permute-start = (bf16[2,128,128]{2,1,0:T(8,128)(2,1)S(1)}, bf16[2,128,128]{2,1,0:T(8,128)(2,1)S(1)}, u32[]{:S(2)}, u32[]{:S(2)}) collective-permute-start(bf16[2,128,128]{2,1,0:T(8,128)(2,1)S(1)} %fusion.76), channel_id=1, source_target_pairs={{0,4},{4,8},{8,12},{1,5},{5,9},{9,13},{2,6},{6,10},{10,14},{3,7},{... | collective-permute-start | bytes 196616 | tf_op jit(solution)/shard_map/while/body/eval_jaxpr/ppermute | solution.py:14
  299.1 5.0 %collective-permute-start = (bf16[2,128,128]{2,1,0:T(8,128)(2,1)S(1)}, bf16[2,128,128]{2,1,0:T(8,128)(2,1)S(1)}, u32[]{:S(2)}, u32[]{:S(2)}) collective-permute-start(bf16[2,128,128]{2,1,0:T(8,128)(2,1)S(1)} %fusion.76), channel_id=1, source_target_pairs={{0,4},{4,8},{8,12},{1,5},{5,9},{9,13},{2,6},{6,10},{10,14},{3,7},{... | collective-permute-start | bytes 196616 | tf_op jit(solution)/shard_map/while/body/eval_jaxpr/ppermute | solution.py:14
  304.4 2.7 copy-start.4
  304.4 2.7 copy-start.5
  307.1 2.4 copy-start.3
  307.1 2.4 copy-start.24
Sparse Core Ops, SparseCore 0:
  310.7 20.8 all-gather.1
where the time goes:
time: 344 us; the launch traced here: 341 us
  other arithmetic  173 us (50%)
  waiting for transfers between devices  48 us (14%)
  local copies, waits for them, and re-layouts  39.4 us (11%)
  matrix products  36.9 us (11%)
  starting transfers between devices  28.6 us (8%)
  between operations  14.6 us (4%)
    another operation x2, other arithmetic, stretch_pieces(): jax.scipy.linalg.solve_triangular(system, right_side, lower=True, unit_di...  159 us
    all_gather x1, waiting for transfers between devices, on_device(): lax.all_gather(normed, 'head', axis=1, tiled=True)  21 us
    dynamic_update_slice x24, local copies, waits for them, and re-layouts, stretch_pieces(): lax.scan(advance, (zero_state, identity_map), (transition.transpose(1, 0,...  11.3 us
    ppermute x3, waiting for transfers between devices, passed_along(): lax.ppermute(value, axis, [(source, source + steps) for source in range(i...  11.1 us
    dot_general x8, matrix products, advance(): jnp.einsum('hde,hef->hdf', step_map, current_state, precision=PRECISE_SET...  9.44 us
    unnamed x62, local copies, waits for them, and re-layouts  8.95 us
  transfers between devices with their start and end apart: 10, of which 9 were waited for; matrix products, arithmetic and copies ran while one was open for 9% of the time, Pallas kernels for 0%

commit v1 on v0

v1 whole, which is shorter than its diff:
```python
import functools

import jax
import jax.numpy as jnp
from jax import lax
from jax.experimental import pallas as pl
from jax.experimental.pallas import tpu as pltpu
from jax.sharding import PartitionSpec as P

F32 = jnp.float32
BF16 = jnp.bfloat16


def mm(a, b):
    return jnp.dot(a.astype(BF16), b.astype(BF16), preferred_element_type=F32)


def mm_nt(a, b):
    return lax.dot_general(
        a.astype(BF16), b.astype(BF16), (((1,), (1,)), ((), ())), preferred_element_type=F32
    )


def mm_tn(a, b):
    return lax.dot_general(
        a.astype(BF16), b.astype(BF16), (((0,), (0,)), ((), ())), preferred_element_type=F32
    )


def iota(shape, dim):
    return lax.broadcasted_iota(jnp.int32, shape, dim)


def unit_lower_inverse(parts, half):
    rows, cols = iota((half, half), 0), iota((half, half), 1)
    size = 1
    inverses = None
    while size < half:
        row_block, col_block = rows // size, cols // size
        link = (row_block == col_block + 1) & (row_block % 2 == 1)
        linked = [jnp.where(link, part, 0.0) for part in parts]
        if inverses is None:
            eye = jnp.where(rows == cols, 1.0, 0.0)
            inverses = [eye - part for part in linked]
        else:
            short = [inverse.astype(BF16) for inverse in inverses]
            middle = [mm(part, inverse) for part, inverse in zip(linked, short)]
            fixes = [mm(inverse, part) for inverse, part in zip(short, middle)]
            inverses = [inverse - fix for inverse, fix in zip(inverses, fixes)]
        size *= 2
    return inverses


def piece_kernel(
    doc_ref,
    query_ref,
    key_ref,
    value_ref,
    rate_ref,
    decay_ref,
    inner_ref,
    carried_ref,
    state_ref,
    *,
    heads_step,
    head_depth,
):
    tokens = query_ref.shape[0]
    steps = 2 * tokens
    half = steps // 2
    heads_all = rate_ref.shape[1]
    docs = doc_ref.shape[0]
    first = (lax.axis_index("seq") * lax.axis_size("head") + lax.axis_index("head")) * tokens

    def doc_of(position):
        return sum((position >= doc_ref[index]).astype(jnp.int32) for index in range(docs))

    doc_before = doc_of(first - 1)
    doc_last = doc_of(first + tokens - 1)
    step_doc_col = doc_of(first + iota((steps, half), 0) // 2)
    step_doc_row = doc_of(first + iota((1, steps), 1) // 2)
    token_doc_col = doc_of(first + iota((tokens, steps), 0))
    col_ids = iota((tokens, steps), 1)
    score_mask = (col_ids <= 2 * iota((tokens, steps), 0) + 1) & (token_doc_col == step_doc_row)
    step_tri = (iota((steps, tokens), 1) <= iota((steps, tokens), 0) // 2).astype(BF16)
    token_tri = (iota((tokens, tokens), 1) <= iota((tokens, tokens), 0)).astype(BF16)
    row_tri = (iota((tokens, steps), 0) <= iota((tokens, steps), 1) // 2).astype(BF16)
    rows, cols = iota((half, half), 0), iota((half, half), 1)
    eye = rows == cols
    lower = rows > cols
    docs_low = step_doc_col[half:] == step_doc_row[:, :half]
    docs_first = (step_doc_col[:half] == step_doc_row[:, :half]) & lower
    docs_second = (step_doc_col[half:] == step_doc_row[:, half:]) & lower
    eye_steps = (iota((steps, steps), 0) == iota((steps, steps), 1)).astype(BF16)

    grams, lefts, work, corners = [], [], [], []
    for local in range(heads_step):
        head = pl.program_id(0) * heads_step + local
        pick = (iota((heads_all, head_depth), 0) == head).astype(BF16)
        lane = slice(local * head_depth, (local + 1) * head_depth)
        query, key, value = query_ref[:, lane], key_ref[:, lane], value_ref[:, lane]
        rate_col = mm(rate_ref[...], pick)
        decay_col = mm(decay_ref[...], pick)
        total_col = mm(step_tri, decay_col)
        token_col = mm(token_tri, decay_col)
        total_row = mm_tn(decay_col, row_tri)[:1]
        rate_row = mm_tn(rate_col, eye_steps)[:1]
        key_one, key_two = key[:half], key[half:]
        gram_one, gram_two = mm_nt(key_one, key_one), mm_nt(key_two, key_two)
        gram_low = mm_nt(key_two, key_one)
        diag_one, diag_two = jnp.where(eye, gram_one, 0.0), jnp.where(eye, gram_two, 0.0)
        inv_row = lax.rsqrt(
            jnp.concatenate(
                [jnp.sum(diag_one, 0, keepdims=True), jnp.sum(diag_two, 0, keepdims=True)], 1
            )
            + 1e-06
        )
        inv_col = lax.rsqrt(
            jnp.concatenate(
                [jnp.sum(diag_one, 1, keepdims=True), jnp.sum(diag_two, 1, keepdims=True)], 0
            )
            + 1e-06
        )
        left = rate_col * inv_col

        def fade(mask, upper, lower_row):
            return jnp.where(mask, jnp.exp(jnp.minimum(upper - lower_row, 0.0)), 0.0)

        part_one = (
            gram_one
            * left[:half]
            * inv_row[:, :half]
            * fade(docs_first, total_col[:half], total_row[:, :half])
        )
        part_two = (
            gram_two
            * left[half:]
            * inv_row[:, half:]
            * fade(docs_second, total_col[half:], total_row[:, half:])
        )
        part_low = (
            gram_low
            * left[half:]
            * inv_row[:, :half]
            * fade(docs_low, total_col[half:], total_row[:, :half])
        )
        grams += [part_one, part_two]
        corners.append(part_low)
        work.append((query, key, value, total_col, token_col, total_row, rate_row, inv_row, inv_col))

    inverses = unit_lower_inverse(grams, half)
    for local in range(heads_step):
        lane = slice(local * head_depth, (local + 1) * head_depth)
        query, key, value, total_col, token_col, total_row, rate_row, inv_row, inv_col = work[local]
        inv_one, inv_two = inverses[2 * local], inverses[2 * local + 1]
        inv_low = -mm(inv_two, mm(corners[local], inv_one))
        start_row = jnp.where(
            step_doc_row == doc_before, jnp.exp(total_row), 0.0
        )
        erase_row = rate_row * start_row * inv_row
        last = total_col[steps - 1 :]
        end_col = jnp.where(step_doc_col == doc_last, jnp.exp(last - total_col), 0.0) * inv_col
        start_token = jnp.where(token_doc_col[:, :half] == doc_before, jnp.exp(token_col), 0.0)

        def solve(scale, right):
            first_rows = mm(inv_one * scale[:, :half], right[:half])
            left = jnp.concatenate([inv_low * scale[:, :half], inv_two * scale[:, half:]], 1)
            return jnp.concatenate([first_rows, mm(left, right)], 0)

        written = solve(rate_row, value)
        erased = solve(erase_row, key)
        token_wide = jnp.concatenate([token_col, token_col], 1)
        scores = mm_nt(query, key) * inv_row * jnp.where(
            score_mask, jnp.exp(jnp.minimum(token_wide - total_row, 0.0)), 0.0
        )
        scores = scores.astype(BF16)
        inner_ref[:, lane] = mm(scores, written)
        carried_ref[:, lane] = (
            start_token * query.astype(F32) - mm(scores, erased)
        ).astype(carried_ref.dtype)
        last_gain = jnp.where(doc_last == doc_before, jnp.exp(last), 0.0)
        state_ref[local, 0] = (jnp.where(eye, last_gain, 0.0) - mm_tn(key, erased * end_col)).astype(
            state_ref.dtype
        )
        state_ref[local, 1] = mm_tn(key, written * end_col).astype(state_ref.dtype)


def local_pieces(queries, keys, values, write_rate, log_decay, doc_starts):
    tokens, width = queries.shape
    heads_all = log_decay.shape[1]
    head_depth = width // heads_all
    heads_step = 2
    lanes = heads_step * head_depth
    steps = 2 * tokens
    return pl.pallas_call(
        functools.partial(piece_kernel, heads_step=heads_step, head_depth=head_depth),
        grid=(heads_all // heads_step,),
        in_specs=[
            pl.BlockSpec(memory_space=pltpu.SMEM),
            pl.BlockSpec((tokens, lanes), lambda i: (0, i)),
            pl.BlockSpec((steps, lanes), lambda i: (0, i)),
            pl.BlockSpec((steps, lanes), lambda i: (0, i)),
            pl.BlockSpec((steps, heads_all), lambda i: (0, 0)),
            pl.BlockSpec((tokens, heads_all), lambda i: (0, 0)),
        ],
        out_specs=[
            pl.BlockSpec((tokens, lanes), lambda i: (0, i)),
            pl.BlockSpec((tokens, lanes), lambda i: (0, i)),
            pl.BlockSpec((heads_step, 2, head_depth, head_depth), lambda i: (i, 0, 0, 0)),
        ],
        out_shape=[
            jax.ShapeDtypeStruct((tokens, width), F32),
            jax.ShapeDtypeStruct((tokens, width), BF16),
            jax.ShapeDtypeStruct((heads_all, 2, head_depth, head_depth), BF16),
        ],
        compiler_params=pltpu.CompilerParams(vmem_limit_bytes=40 * 1024 * 1024),
        name="pieces",
    )(
        doc_starts,
        queries,
        keys.reshape(steps, width),
        values.reshape(steps, width),
        write_rate.reshape(steps, heads_all),
        log_decay,
    )


def passed_along(value, axis, steps):
    count = lax.axis_size(axis)
    return lax.ppermute(value, axis, [(source, source + steps) for source in range(count - steps)])


def on_device(
    queries, keys, values, out_gate, write_rate, log_decay, doc_starts, norm_gain, out_weight
):
    tokens, width = queries.shape
    heads_all = log_decay.shape[1]
    head_depth = width // heads_all
    groups = lax.axis_size("head")
    inner, carried, states = local_pieces(
        queries, keys, values, write_rate, log_decay, doc_starts
    )
    mine = lax.all_to_all(states, "head", split_axis=0, concat_axis=0, tiled=True)
    mine = mine.reshape(groups, heads_all // groups, 2, head_depth, head_depth)

    def step(maps, state, index):
        return jnp.einsum(
            "hde,hef->hdf", maps, state.astype(BF16), preferred_element_type=F32
        ) + mine[index, :, 1].astype(F32)

    def sweep(incoming):
        states_in = [incoming]
        for index in range(groups):
            states_in.append(step(mine[index, :, 0], states_in[-1], index))
        return states_in

    incoming = jnp.zeros(mine.shape[1:2] + mine.shape[3:], F32)
    for _ in range(lax.axis_size("seq") // 2):
        incoming = passed_along(sweep(incoming)[-1].astype(BF16), "seq", 1).astype(F32)
    starts = jnp.stack(sweep(incoming)[:groups]).astype(BF16)
    starts = starts.reshape(heads_all, head_depth, head_depth)
    back = lax.all_to_all(starts, "head", split_axis=0, concat_axis=0, tiled=True)
    readout = inner.reshape(tokens, heads_all, head_depth) + jnp.einsum(
        "thd,hde->the",
        carried.reshape(tokens, heads_all, head_depth),
        back,
        preferred_element_type=F32,
    )
    gate_vals = out_gate.reshape(tokens, heads_all, head_depth).astype(F32)
    inv_rms = lax.rsqrt(jnp.mean(readout * readout, -1, keepdims=True) + 1e-05)
    normed = (readout * inv_rms * norm_gain * jax.nn.silu(gate_vals)).astype(BF16)
    normed = normed.reshape(tokens, width)
    acc_total = jnp.dot(
        lax.all_gather(normed, "head", axis=0, tiled=True), out_weight, preferred_element_type=F32
    )
    return acc_total.astype(BF16)


def solution(mesh):
    placed = (
        P(("rep", "seq", "head"), None),
        P(("rep", "seq", "head"), None, None),
        P(("rep", "seq", "head"), None, None),
        P(("rep", "seq", "head"), None),
        P(("rep", "seq", "head"), None, None),
        P(("rep", "seq", "head"), None),
        P("rep"),
        P(),
        P(None, "head"),
    )
    return jax.shard_map(
        on_device, mesh=mesh, in_specs=placed, out_specs=P(("rep", "seq"), "head"), check_vma=False
    )
```

time: 344 us -> 91.7 us (0.27)
  other arithmetic: 173 us -> 0.94 us
  local copies, waits for them, and re-layouts: 39.4 us -> 5.91 us
  matrix products: 36.9 us -> 4.71 us
  starting transfers between devices: 28.6 us -> 9.28 us
  waiting for transfers between devices: 48 us -> 29.1 us
  Pallas kernels: 0 us -> 15.5 us
  blocking collectives: 0 us -> 11 us
    another operation x5 -> x1, other arithmetic: 159 us -> 0.04 us  [on_device(): starts = jnp.stack(sweep(incoming)[:groups]).astype(BF16)]
    dot_general x28 -> x9, matrix products: 34.9 us -> 4.71 us  [the longest x1 2.75 us: on_device(): jnp.dot(lax.all_gather(normed, 'head', axis=0, tiled=True), out_weight, p...]
    all_to_all x6 -> x1, starting transfers between devices: 24.8 us -> 6.7 us  [on_device(): lax.all_to_all(starts, 'head', split_axis=0, concat_axis=0, tiled=True)]
    pallas_call x0 -> x1, Pallas kernels: none -> 15.5 us  [local_pieces(): pl.pallas_call(functools.partial(piece_kernel, heads_step=heads_step, hea...]
    all_to_all x6 -> x1, waiting for transfers between devices: 15.9 us -> 4.03 us  [on_device(): lax.all_to_all(starts, 'head', split_axis=0, concat_axis=0, tiled=True)]
    dynamic_update_slice x24 -> x0, local copies, waits for them, and re-layouts: 11.3 us -> none  [stretch_pieces(): lax.scan(advance, (zero_state, identity_map), (transition.transpose(1, 0,...]
    all_to_all x0 -> x1, blocking collectives: none -> 11 us  [on_device(): lax.all_to_all(states, 'head', split_axis=0, concat_axis=0, tiled=True)]
    unnamed x62 -> x18, local copies, waits for them, and re-layouts: 8.95 us -> 2.43 us
  transfers between devices with their start and end apart: 10 -> 4, of which waited for: 9 -> 4; matrix products, arithmetic and copies ran while one was open for 9% -> 1% of each run, Pallas kernels for 0% -> 0%
where the time goes in v1:
time: 91.7 us; the launch traced here: 90 us
  waiting for transfers between devices  29.1 us (32%)
  Pallas kernels  15.5 us (17%)
  between operations  13.5 us (15%)
  blocking collectives  11 us (12%)
  starting transfers between devices  9.28 us (10%)
  local copies, waits for them, and re-layouts  5.91 us (6%)
  matrix products  4.71 us (5%)
  other arithmetic  0.94 us (1%)
    all_gather x1, waiting for transfers between devices, on_device(): lax.all_gather(normed, 'head', axis=0, tiled=True)  17.7 us
    pallas_call x1, Pallas kernels, local_pieces(): pl.pallas_call(functools.partial(piece_kernel, heads_step=heads_step, hea...  15.5 us
    all_to_all x1, blocking collectives, on_device(): lax.all_to_all(states, 'head', split_axis=0, concat_axis=0, tiled=True)  11 us
    ppermute x2, waiting for transfers between devices, passed_along(): lax.ppermute(value, axis, [(source, source + steps) for source in range(c...  7.42 us
    all_to_all x1, starting transfers between devices, on_device(): lax.all_to_all(starts, 'head', split_axis=0, concat_axis=0, tiled=True)  6.7 us
    all_to_all x1, waiting for transfers between devices, on_device(): lax.all_to_all(starts, 'head', split_axis=0, concat_axis=0, tiled=True)  4.03 us
    dot_general x1, matrix products, on_device(): jnp.dot(lax.all_gather(normed, 'head', axis=0, tiled=True), out_weight, p...  2.75 us
    ppermute x2, starting transfers between devices, passed_along(): lax.ppermute(value, axis, [(source, source + steps) for source in range(c...  2.58 us
  transfers between devices with their start and end apart: 4, of which 4 were waited for; matrix products, arithmetic and copies ran while one was open for 1% of the time, Pallas kernels for 0%

profile of v1, /device:TPU:25, one launch (start us, length us, event | category | flops | bytes accessed | tf_op | source)
XLA Modules:
  0.0 90.0 jit_solution(1160564532510110824)
XLA Ops:
  6.5 0.0 copy-start
  6.5 0.0 copy-start.6
  6.5 0.9 %copy.11.decay_ref = bf16[128,8]{1,0:T(8,128)(2,1)S(1)} copy(bf16[128,8]{0,1:T(8,128)(2,1)} %param.14) | data formatting | bytes 4096 | tf_op args[5]
  7.4 0.0 copy-done.6
  7.4 0.1 copy.10
  7.6 0.0 copy-start.4
  7.6 1.3 %reshape.44.key_ref = bf16[256,1024]{1,0:T(8,128)(2,1)S(1)} reshape(bf16[128,2,1024]{2,1,0:T(2,128)(2,1)} %param.10) | data formatting | bytes 1048576 | tf_op jit(solution)/shard_map/reshape | solution.py:221
  8.9 0.0 copy-done.4
  8.9 0.0 copy-start.1
  8.9 0.2 reshape.45.value_ref
  9.1 0.0 copy-start.2
  9.1 0.7 copy-done.1
  9.9 0.0 copy-done.2
  9.9 15.5 %pieces.1 = (f32[128,1024]{1,0:T(8,128)S(1)}, bf16[128,1024]{1,0:T(8,128)(2,1)S(1)}, bf16[8,2,128,128]{3,2,1,0:T(8,128)(2,1)S(1)}) custom-call(s32[4]{0:T(128)S(1)} %copy-done.2, bf16[128,1024]{1,0:T(8,128)(2,1)S(1)} %copy-done.1, bf16[256,1024]{1,0:T(8,128)(2,1)S(1)} %reshape.44.key_ref, bf16[256,1024]{1,0:T(8,128)(2,1)S(1)} %reshape.45.value_ref, ...), custom_call_target="tpu_custom_call" | custom-call | tf_op jit(solution)/shard_map/pieces/pallas_call | solution.py:195
  25.4 11.0 %all_to_all.10 = bf16[8,2,128,128]{3,2,1,0:T(8,128)(2,1)S(1)} all-to-all(bf16[8,2,128,128]{3,2,1,0:T(8,128)(2,1)S(1)} %get-tuple-element.9), channel_id=1, replica_groups=mesh['rep'=2,'seq'=4,'head'=4] {'head'}, dimensions={0} | all-to-all | bytes 1048576 | tf_op jit(solution)/shard_map/all_to_all | solution.py:243
  36.4 0.3 fusion.2
  36.7 0.3 fusion.4
  37.0 1.3 %collective-permute-start = (bf16[2,128,128]{2,1,0:T(8,128)(2,1)S(1)}, bf16[2,128,128]{2,1,0:T(8,128)(2,1)S(1)}, u32[]{:S(2)}, u32[]{:S(2)}) collective-permute-start(bf16[2,128,128]{2,1,0:T(8,128)(2,1)S(1)} %fusion.4), channel_id=1, source_target_pairs={{0,4},{4,8},{8,12},{1,5},{5,9},{9,13},{2,6},{6,10},{10,14},{3,7},{... | collective-permute-start | bytes 196616 | tf_op jit(solution)/shard_map/ppermute | solution.py:230
  38.3 3.7 %collective-permute-done = bf16[2,128,128]{2,1,0:T(8,128)(2,1)S(1)} collective-permute-done((bf16[2,128,128]{2,1,0:T(8,128)(2,1)S(1)}, bf16[2,128,128]{2,1,0:T(8,128)(2,1)S(1)}, u32[]{:S(2)}, u32[]{:S(2)}) %collective-permute-start) | collective-permute-done | bytes 65568 | tf_op jit(solution)/shard_map/ppermute | solution.py:230
  42.0 0.3 fusion.6
  42.3 0.3 fusion.8
  42.6 1.3 %collective-permute-start.1 = (bf16[2,128,128]{2,1,0:T(8,128)(2,1)S(1)}, bf16[2,128,128]{2,1,0:T(8,128)(2,1)S(1)}, u32[]{:S(2)}, u32[]{:S(2)}) collective-permute-start(bf16[2,128,128]{2,1,0:T(8,128)(2,1)S(1)} %fusion.8), channel_id=1, source_target_pairs={{0,4},{4,8},{8,12},{1,5},{5,9},{9,13},{2,6},{6,10},{10,14},{3,7},{... | collective-permute-start | bytes 196616 | tf_op jit(solution)/shard_map/ppermute | solution.py:230
  43.9 3.7 %collective-permute-done.1 = bf16[2,128,128]{2,1,0:T(8,128)(2,1)S(1)} collective-permute-done((bf16[2,128,128]{2,1,0:T(8,128)(2,1)S(1)}, bf16[2,128,128]{2,1,0:T(8,128)(2,1)S(1)}, u32[]{:S(2)}, u32[]{:S(2)}) %collective-permute-start.1) | collective-permute-done | bytes 65568 | tf_op jit(solution)/shard_map/ppermute | solution.py:230
  47.6 0.2 fusion.9
  47.7 0.2 fusion.10
  47.9 0.2 fusion.12
  48.1 0.9 copy.20
  49.0 6.7 %all-to-all-start.1 = ((bf16[8,128,128]{1,2,0:T(8,128)(2,1)}), bf16[8,128,128]{1,2,0:T(8,128)(2,1)S(1)}, u32[]{:S(2)}, u32[]{:S(2)}) async-start(bf16[8,128,128]{1,2,0:T(8,128)(2,1)} %copy.20), calls=%async_computation.1 | async-start | bytes 524288 | tf_op jit(solution)/shard_map/all_to_all | solution.py:262
  55.7 0.0 all-gather.2.cloned.1.call-start
  55.7 0.0 copy-start.5
  55.7 1.0 %copy.24 = f32[128,1024]{0,1:T(8,128)} copy(f32[128,1024]{1,0:T(8,128)S(1)} %get-tuple-element.8) | data formatting | bytes 1048576 | tf_op jit(solution)/shard_map/reshape | solution.py:263
  56.7 0.0 copy-done.5
  56.7 0.0 copy-start.3
  56.7 0.1 copy.23
  56.8 4.0 %all-to-all-done.1 = bf16[8,128,128]{1,2,0:T(8,128)(2,1)S(1)} async-done(((bf16[8,128,128]{1,2,0:T(8,128)(2,1)}), bf16[8,128,128]{1,2,0:T(8,128)(2,1)S(1)}, u32[]{:S(2)}, u32[]{:S(2)}) %all-to-all-start.1) | async-done | bytes 262176 | tf_op jit(solution)/shard_map/all_to_all | solution.py:262
  60.8 0.0 copy-done.3
  60.8 0.3 multiply_reduce_fusion
  61.2 0.0 copy-start.7
  61.2 0.6 copy-done.7
  61.8 0.9 multiply_convert_fusion
  62.7 0.0 all-gather.2.cloned.1.call-update
  62.7 17.7 %all-gather.2.cloned.1.call-done = bf16[512,1024]{0,1:T(8,128)(2,1)} async-done(((bf16[128,1024]{0,1:T(8,128)(2,1)}), bf16[512,1024]{0,1:T(8,128)(2,1)}) %all-gather.2.cloned.1.call-update) | async-done | bytes 1048592 | tf_op jit(solution)/shard_map/all_gather | solution.py:274
  80.4 0.0 copy-done
  80.4 2.7 %convolution_convert_fusion = bf16[512,512]{1,0:T(8,128)(2,1)} fusion(bf16[512,1024]{0,1:T(8,128)(2,1)} %all-gather.2.cloned.1.call-done, bf16[1024,512]{1,0:T(8,128)(2,1)S(1)} %copy-done), kind=kOutput, calls=%fused_computation | convolution fusion | flops 537133056 | bytes 2621440 | tf_op jit(solution)/shard_map/dot_general | solution.py:273
  (2 shorter events, 0.0 us)
Async XLA Ops:
  6.5 73.9 %copy-start = (bf16[1024,512]{1,0:T(8,128)(2,1)S(1)}, bf16[1024,512]{1,0:T(8,128)(2,1)}, u32[]{:S(2)}) copy-start(bf16[1024,512]{1,0:T(8,128)(2,1)} %param.17) | copy-start | bytes 3145732
  6.5 0.9 %copy-start.6 = (bf16[128,2,8]{0,2,1:T(8,128)(2,1)S(1)}, bf16[128,2,8]{0,2,1:T(8,128)(2,1)}, u32[]{:S(2)}) copy-start(bf16[128,2,8]{0,2,1:T(8,128)(2,1)} %param.13) | copy-start | bytes 12292
  7.6 1.3 %copy-start.4 = (bf16[128,2,1024]{2,1,0:T(2,128)(2,1)S(1)}, bf16[128,2,1024]{2,1,0:T(2,128)(2,1)}, u32[]{:S(2)}) copy-start(bf16[128,2,1024]{2,1,0:T(2,128)(2,1)} %param.11) | copy-start | bytes 1572868
  8.9 1.0 %copy-start.1 = (bf16[128,1024]{1,0:T(8,128)(2,1)S(1)}, bf16[128,1024]{1,0:T(8,128)(2,1)}, u32[]{:S(2)}) copy-start(bf16[128,1024]{1,0:T(8,128)(2,1)} %query_ref.1) | copy-start | bytes 786436
  9.1 0.7 copy-start.2
  37.0 5.0 %collective-permute-start = (bf16[2,128,128]{2,1,0:T(8,128)(2,1)S(1)}, bf16[2,128,128]{2,1,0:T(8,128)(2,1)S(1)}, u32[]{:S(2)}, u32[]{:S(2)}) collective-permute-start(bf16[2,128,128]{2,1,0:T(8,128)(2,1)S(1)} %fusion.4), channel_id=1, source_target_pairs={{0,4},{4,8},{8,12},{1,5},{5,9},{9,13},{2,6},{6,10},{10,14},{3,7},{... | collective-permute-start | bytes 196616 | tf_op jit(solution)/shard_map/ppermute | solution.py:230
  42.6 5.0 %collective-permute-start.1 = (bf16[2,128,128]{2,1,0:T(8,128)(2,1)S(1)}, bf16[2,128,128]{2,1,0:T(8,128)(2,1)S(1)}, u32[]{:S(2)}, u32[]{:S(2)}) collective-permute-start(bf16[2,128,128]{2,1,0:T(8,128)(2,1)S(1)} %fusion.8), channel_id=1, source_target_pairs={{0,4},{4,8},{8,12},{1,5},{5,9},{9,13},{2,6},{6,10},{10,14},{3,7},{... | collective-permute-start | bytes 196616 | tf_op jit(solution)/shard_map/ppermute | solution.py:230
  49.0 11.9 %all-to-all-start.1 = ((bf16[8,128,128]{1,2,0:T(8,128)(2,1)}), bf16[8,128,128]{1,2,0:T(8,128)(2,1)S(1)}, u32[]{:S(2)}, u32[]{:S(2)}) async-start(bf16[8,128,128]{1,2,0:T(8,128)(2,1)} %copy.20), calls=%async_computation.1 | async-start | bytes 524288 | tf_op jit(solution)/shard_map/all_to_all | solution.py:262
  55.7 24.7 %all-gather.2.cloned.1.call-start = ((), (), s32[]{:S(2)}) async-start(), calls=%async_computation.2 | async-start | bytes 1310720 | tf_op jit(solution)/shard_map/all_gather | solution.py:274
  55.7 1.0 %copy-start.5 = (bf16[128,1024]{1,0:T(8,128)(2,1)S(1)}, bf16[128,1024]{1,0:T(8,128)(2,1)}, u32[]{:S(2)}) copy-start(bf16[128,1024]{1,0:T(8,128)(2,1)} %param.12) | copy-start | bytes 786436
  56.7 4.2 %copy-start.3 = (f32[128,1024]{0,1:T(8,128)S(1)}, f32[128,1024]{0,1:T(8,128)}, u32[]{:S(2)}) copy-start(f32[128,1024]{0,1:T(8,128)} %copy.24) | copy-start | bytes 1572868
  61.2 0.7 copy-start.7
Sparse Core Ops, SparseCore 0:
  62.9 17.4 all-gather.1

commit v2 on v1

--- a/solution.py
+++ b/solution.py
@@ -225,9 +225,215 @@
     )
 
 
-def passed_along(value, axis, steps):
-    count = lax.axis_size(axis)
-    return lax.ppermute(value, axis, [(source, source + steps) for source in range(count - steps)])
+MESH = pl.DeviceIdType.MESH
+
+
+def join_kernel(
+    inner_ref,
+    carried_ref,
+    state_ref,
+    gate_ref,
+    gain_ref,
+    weight_ref,
+    out_ref,
+    mine,
+    relay_out,
+    relay_in,
+    starts,
+    back,
+    normed,
+    deal_send,
+    deal_recv,
+    relay_send,
+    relay_recv,
+    back_send,
+    back_recv,
+    far_send,
+    far_recv,
+    near_send,
+    near_recv,
+):
+    groups, heads_here, _, depth, _ = mine.shape
+    hops = relay_in.shape[0]
+    tokens = inner_ref.shape[0]
+    block = heads_here * depth
+    me, place, places = lax.axis_index("head"), lax.axis_index("seq"), lax.axis_size("seq")
+    has_next, has_prior = place < places - 1, place > 0
+    chips = groups // 2
+    sibling = me + 1 - 2 * lax.rem(me, 2)
+
+    def to_head(source, target, send, recv, peer):
+        return pltpu.make_async_remote_copy(
+            src_ref=source,
+            dst_ref=target,
+            send_sem=send,
+            recv_sem=recv,
+            device_id={"head": peer},
+            device_id_type=MESH,
+        )
+
+    barrier = pltpu.get_barrier_semaphore()
+    for offset in range(1, groups):
+        pl.semaphore_signal(
+            barrier, inc=1, device_id={"head": lax.rem(me + offset, groups)}, device_id_type=MESH
+        )
+
+    @pl.when(has_next)
+    def _():
+        pl.semaphore_signal(barrier, inc=1, device_id={"seq": place + 1}, device_id_type=MESH)
+
+    @pl.when(has_prior)
+    def _():
+        pl.semaphore_signal(barrier, inc=1, device_id={"seq": place - 1}, device_id_type=MESH)
+
+    pl.semaphore_wait(
+        barrier, groups - 1 + has_next.astype(jnp.int32) + has_prior.astype(jnp.int32)
+    )
+
+    deals = []
+    for offset in range(1, groups):
+        peer = lax.rem(me + offset, groups)
+        copy = to_head(
+            state_ref.at[pl.ds(peer * heads_here, heads_here)],
+            mine.at[me],
+            deal_send.at[offset],
+            deal_recv.at[offset],
+            peer,
+        )
+        copy.start()
+        deals.append(copy)
+    mine[me] = state_ref[pl.ds(me * heads_here, heads_here)]
+
+    @pl.when(place == 0)
+    def _():
+        relay_in[...] = jnp.zeros_like(relay_in)
+
+    for copy in deals:
+        copy.wait_recv()
+
+    sums, maps = [], []
+    for local in range(heads_here):
+        chain = [None, mine[0, local, 1].astype(F32)]
+        for index in range(1, groups):
+            chain.append(
+                mm(mine[index, local, 0], chain[-1]) + mine[index, local, 1].astype(F32)
+            )
+        sums.append(chain)
+
+    def relay(hop):
+        return pltpu.make_async_remote_copy(
+            src_ref=relay_out.at[hop],
+            dst_ref=relay_in.at[hop],
+            send_sem=relay_send.at[hop],
+            recv_sem=relay_recv.at[hop],
+            device_id={"seq": place + 1},
+            device_id_type=MESH,
+        )
+
+    for hop in range(hops):
+        for local in range(heads_here):
+            value = sums[local][groups]
+            if hop:
+                value = value + mm(maps[local][groups], relay_in[hop - 1, local])
+            relay_out[hop, local] = value.astype(BF16)
+
+        @pl.when(has_next)
+        def _(hop=hop):
+            relay(hop).start()
+
+        if hop == 0:
+            for local in range(heads_here):
+                chain = [None, mine[0, local, 0]]
+                for index in range(1, groups):
+                    chain.append(mm(mine[index, local, 0], chain[-1]).astype(BF16))
+                maps.append(chain)
+
+        @pl.when(has_prior)
+        def _(hop=hop):
+            relay(hop).wait_recv()
+
+    for local in range(heads_here):
+        incoming = relay_in[hops - 1, local]
+        starts[0, local] = incoming
+        for index in range(1, groups):
+            starts[index, local] = (
+                mm(maps[local][index], incoming) + sums[local][index]
+            ).astype(BF16)
+    returns = []
+    for offset in range(1, groups):
+        peer = lax.rem(me + offset, groups)
+        copy = to_head(
+            starts.at[peer], back.at[me], back_send.at[offset], back_recv.at[offset], peer
+        )
+        copy.start()
+        returns.append(copy)
+    back[me] = starts[me]
+
+    gain = gain_ref[...]
+    fars, nears = [], []
+    for piece in range(groups):
+        if piece:
+            returns[piece - 1].wait_recv()
+        owner = lax.rem(me - piece + groups, groups)
+        for local in range(heads_here):
+            lanes = pl.ds(pl.multiple_of(owner * block + local * depth, depth), depth)
+            readout = inner_ref[:, lanes] + mm(carried_ref[:, lanes], back[owner, local])
+            gate = gate_ref[:, lanes].astype(F32)
+            inv_rms = lax.rsqrt(jnp.mean(readout * readout, -1, keepdims=True) + 1e-05)
+            normed[me, :, lanes] = (
+                readout * inv_rms * gain * (gate / (1.0 + jnp.exp(-gate)))
+            ).astype(BF16)
+        lanes = pl.ds(pl.multiple_of(owner * block, block), block)
+        here = normed.at[me, :, lanes]
+        for chip in range(1, chips):
+            copy = to_head(
+                here,
+                here,
+                far_send.at[piece, chip],
+                far_recv.at[piece, chip],
+                lax.rem(me + 2 * chip, groups),
+            )
+            copy.start()
+            fars.append((chip, piece, copy))
+        copy = to_head(here, here, near_send.at[piece, 0], near_recv.at[piece, 0], sibling)
+        copy.start()
+        nears.append(copy)
+
+    def project(source):
+        rows = pl.ds(pl.multiple_of(source * tokens, tokens), tokens)
+        out_ref[rows, :] = jnp.dot(
+            normed[source], weight_ref[...], preferred_element_type=F32
+        ).astype(out_ref.dtype)
+
+    project(me)
+    forwards = []
+    for chip, piece, copy in fars:
+        source = lax.rem(me - 2 * chip + groups, groups)
+        owner = lax.rem(source - piece + groups, groups)
+        there = normed.at[source, :, pl.ds(pl.multiple_of(owner * block, block), block)]
+        copy.wait_recv()
+        onward = to_head(
+            there, there, near_send.at[piece, chip], near_recv.at[piece, chip], sibling
+        )
+        onward.start()
+        forwards.append(onward)
+    for copy in nears:
+        copy.wait_recv()
+    project(sibling)
+    for chip in range(1, chips):
+        project(lax.rem(me - 2 * chip + groups, groups))
+    for onward in forwards:
+        onward.wait_recv()
+    for chip in range(1, chips):
+        project(lax.rem(sibling - 2 * chip + groups, groups))
+
+    for copy in deals + returns + [far[2] for far in fars] + nears + forwards:
+        copy.wait_send()
+    for hop in range(hops):
+
+        @pl.when(has_next)
+        def _(hop=hop):
+            relay(hop).wait_send()
 
 
 def on_device(
@@ -235,45 +441,42 @@
 ):
     tokens, width = queries.shape
     heads_all = log_decay.shape[1]
-    head_depth = width // heads_all
+    depth = width // heads_all
     groups = lax.axis_size("head")
+    heads_here = heads_all // groups
+    hops = lax.axis_size("seq") // 2
     inner, carried, states = local_pieces(
         queries, keys, values, write_rate, log_decay, doc_starts
     )
-    mine = lax.all_to_all(states, "head", split_axis=0, concat_axis=0, tiled=True)
-    mine = mine.reshape(groups, heads_all // groups, 2, head_depth, head_depth)
-
-    def step(maps, state, index):
-        return jnp.einsum(
-            "hde,hef->hdf", maps, state.astype(BF16), preferred_element_type=F32
-        ) + mine[index, :, 1].astype(F32)
-
-    def sweep(incoming):
-        states_in = [incoming]
-        for index in range(groups):
-            states_in.append(step(mine[index, :, 0], states_in[-1], index))
-        return states_in
-
-    incoming = jnp.zeros(mine.shape[1:2] + mine.shape[3:], F32)
-    for _ in range(lax.axis_size("seq") // 2):
-        incoming = passed_along(sweep(incoming)[-1].astype(BF16), "seq", 1).astype(F32)
-    starts = jnp.stack(sweep(incoming)[:groups]).astype(BF16)
-    starts = starts.reshape(heads_all, head_depth, head_depth)
-    back = lax.all_to_all(starts, "head", split_axis=0, concat_axis=0, tiled=True)
-    readout = inner.reshape(tokens, heads_all, head_depth) + jnp.einsum(
-        "thd,hde->the",
-        carried.reshape(tokens, heads_all, head_depth),
-        back,
-        preferred_element_type=F32,
-    )
-    gate_vals = out_gate.reshape(tokens, heads_all, head_depth).astype(F32)
-    inv_rms = lax.rsqrt(jnp.mean(readout * readout, -1, keepdims=True) + 1e-05)
-    normed = (readout * inv_rms * norm_gain * jax.nn.silu(gate_vals)).astype(BF16)
-    normed = normed.reshape(tokens, width)
-    acc_total = jnp.dot(
-        lax.all_gather(normed, "head", axis=0, tiled=True), out_weight, preferred_element_type=F32
-    )
-    return acc_total.astype(BF16)
+    sems = pltpu.SemaphoreType.DMA
+    return pl.pallas_call(
+        join_kernel,
+        in_specs=[pl.BlockSpec(memory_space=pltpu.VMEM)] * 6,
+        out_specs=pl.BlockSpec(memory_space=pltpu.VMEM),
+        out_shape=jax.ShapeDtypeStruct((groups * tokens, out_weight.shape[1]), BF16),
+        scratch_shapes=[
+            pltpu.VMEM((groups, heads_here, 2, depth, depth), BF16),
+            pltpu.VMEM((hops, heads_here, depth, depth), BF16),
+            pltpu.VMEM((hops, heads_here, depth, depth), BF16),
+            pltpu.VMEM((groups, heads_here, depth, depth), BF16),
+            pltpu.VMEM((groups, heads_here, depth, depth), BF16),
+            pltpu.VMEM((groups, tokens, width), BF16),
+            sems((groups,)),
+            sems((groups,)),
+            sems((hops,)),
+            sems((hops,)),
+            sems((groups,)),
+            sems((groups,)),
+            sems((groups, groups // 2)),
+            sems((groups, groups // 2)),
+            sems((groups, groups // 2)),
+            sems((groups, groups // 2)),
+        ],
+        compiler_params=pltpu.CompilerParams(
+            collective_id=0, has_side_effects=True, vmem_limit_bytes=40 * 1024 * 1024
+        ),
+        name="join",
+    )(inner, carried, states, out_gate, norm_gain.reshape(1, depth), out_weight)
 
 
 def solution(mesh):

time: 91.7 us -> 46.1 us (0.50); the launches traced: 90 us -> 45.8 us
  waiting for transfers between devices: 29.1 us -> 0 us
  Pallas kernels: 15.5 us -> 41.7 us
  between operations: 13.5 us -> 0.12 us
  blocking collectives: 11 us -> 0 us
  starting transfers between devices: 9.28 us -> 0 us
  matrix products: 4.71 us -> 0 us
  local copies, waits for them, and re-layouts: 5.91 us -> 3.91 us
  other arithmetic: 0.94 us -> 0 us
    pallas_call x0 -> x1, Pallas kernels: none -> 26.2 us  [on_device(): pl.pallas_call(join_kernel, in_specs=[pl.BlockSpec(memory_space=pltpu.VME...]
    all_gather x1 -> x0, waiting for transfers between devices: 17.7 us -> none  [on_device(): lax.all_gather(normed, 'head', axis=0, tiled=True)]
    all_to_all x1 -> x0, blocking collectives: 11 us -> none  [on_device(): lax.all_to_all(states, 'head', split_axis=0, concat_axis=0, tiled=True)]
    ppermute x2 -> x0, waiting for transfers between devices: 7.42 us -> none  [passed_along(): lax.ppermute(value, axis, [(source, source + steps) for source in range(c...]
    all_to_all x1 -> x0, starting transfers between devices: 6.7 us -> none  [on_device(): lax.all_to_all(starts, 'head', split_axis=0, concat_axis=0, tiled=True)]
    dot_general x9 -> x0, matrix products: 4.71 us -> none  [the longest x1 2.75 us: on_device(): jnp.dot(lax.all_gather(normed, 'head', axis=0, tiled=True), out_weight, p...]
    all_to_all x1 -> x0, waiting for transfers between devices: 4.03 us -> none  [on_device(): lax.all_to_all(starts, 'head', split_axis=0, concat_axis=0, tiled=True)]
    ppermute x2 -> x0, starting transfers between devices: 2.58 us -> none  [passed_along(): lax.ppermute(value, axis, [(source, source + steps) for source in range(c...]
  transfers between devices with their start and end apart: 4 -> 0, of which waited for: 4 -> 0; matrix products, arithmetic and copies ran while one was open for 1% -> 0% of each run, Pallas kernels for 0% -> 0%
where the time goes in v2:
time: 46.1 us; the launch traced here: 45.8 us
  Pallas kernels  41.7 us (90%)
  local copies, waits for them, and re-layouts  3.91 us (8%)
    pallas_call x1, Pallas kernels, on_device(): pl.pallas_call(join_kernel, in_specs=[pl.BlockSpec(memory_space=pltpu.VME...  26.2 us
    pallas_call x1, Pallas kernels, local_pieces(): pl.pallas_call(functools.partial(piece_kernel, heads_step=heads_step, hea...  15.5 us
    unnamed x17, local copies, waits for them, and re-layouts  2.4 us
    reshape x1, local copies, waits for them, and re-layouts, local_pieces(): keys.reshape(steps, width)  1.31 us

profile of v2, /device:TPU:25, one launch (start us, length us, event | category | flops | bytes accessed | tf_op | source)
XLA Modules:
  0.0 45.8 jit_solution(2988210354034582583)
XLA Ops:
  0.0 0.0 copy-start.6
  0.0 0.8 %copy.11.decay_ref = bf16[128,8]{1,0:T(8,128)(2,1)S(1)} copy(bf16[128,8]{0,1:T(8,128)(2,1)} %param.14) | data formatting | bytes 4096 | tf_op args[5]
  0.8 0.0 copy-done.6
  0.8 0.1 copy.10
  0.9 0.0 copy-start.5
  1.0 0.0 copy-start.1
  1.0 0.0 copy-start.3
  1.0 1.3 %reshape.12.key_ref = bf16[256,1024]{1,0:T(8,128)(2,1)S(1)} reshape(bf16[128,2,1024]{2,1,0:T(2,128)(2,1)} %param.10) | data formatting | bytes 1048576 | tf_op jit(solution)/shard_map/reshape | solution.py:221
  2.3 0.0 copy-done.5
  2.3 0.0 copy-start
  2.3 0.2 reshape.13.value_ref
  2.5 0.0 copy-done.1
  2.5 0.0 copy-done.3
  2.5 0.0 copy-start.2
  2.6 15.5 %pieces.1 = (f32[128,1024]{1,0:T(8,128)S(1)}, bf16[128,1024]{1,0:T(8,128)(2,1)S(1)}, bf16[8,2,128,128]{3,2,1,0:T(8,128)(2,1)S(1)}) custom-call(s32[4]{0:T(128)S(1)} %copy-done.3, bf16[128,1024]{1,0:T(8,128)(2,1)S(1)} %copy-done.1, bf16[256,1024]{1,0:T(8,128)(2,1)S(1)} %reshape.12.key_ref, bf16[256,1024]{1,0:T(8,128)(2,1)S(1)} %reshape.13.value_ref, ...), custom_call_target="tpu_custom_call" | custom-call | tf_op jit(solution)/shard_map/pieces/pallas_call | solution.py:195
  18.1 0.0 copy-start.4
  18.1 0.0 copy-done
  18.1 0.0 copy-done.2
  18.1 0.6 %copy-done.4 = f32[128]{0:T(128)S(1)} copy-done((f32[128]{0:T(128)S(1)}, f32[128]{0:T(128)}, u32[]{:S(2)}) %copy-start.4) | copy-done | bytes 536
  18.7 26.2 %join.1 = bf16[512,512]{1,0:T(8,128)(2,1)S(1)} custom-call(f32[128,1024]{1,0:T(8,128)S(1)} %get-tuple-element.8.inner_ref, bf16[128,1024]{1,0:T(8,128)(2,1)S(1)} %get-tuple-element.9.carried_ref, bf16[8,2,128,128]{3,2,1,0:T(8,128)(2,1)S(1)} %get-tuple-element.10.state_ref, bf16[128,1024]{1,0:T(8,128)(2,1)S(1)} %copy-done.2, f32[1,128]{1,0:T(1,128)S(1)} %bitcast.3, ...), custom_call_target="tpu_custom_call" | custom-call | tf_op jit(solution)/shard_map/join/pallas_call | solution.py:452
  45.0 0.8 %copy.13 = bf16[512,512]{1,0:T(8,128)(2,1)} copy(bf16[512,512]{1,0:T(8,128)(2,1)S(1)} %join.1) | data formatting | bytes 1048576
Async XLA Ops:
  0.0 0.8 %copy-start.6 = (bf16[128,2,8]{0,2,1:T(8,128)(2,1)S(1)}, bf16[128,2,8]{0,2,1:T(8,128)(2,1)}, u32[]{:S(2)}) copy-start(bf16[128,2,8]{0,2,1:T(8,128)(2,1)} %param.13) | copy-start | bytes 12292
  0.9 1.4 %copy-start.5 = (bf16[128,2,1024]{2,1,0:T(2,128)(2,1)S(1)}, bf16[128,2,1024]{2,1,0:T(2,128)(2,1)}, u32[]{:S(2)}) copy-start(bf16[128,2,1024]{2,1,0:T(2,128)(2,1)} %param.11) | copy-start | bytes 1572868
  1.0 1.6 %copy-start.1 = (bf16[128,1024]{1,0:T(8,128)(2,1)S(1)}, bf16[128,1024]{1,0:T(8,128)(2,1)}, u32[]{:S(2)}) copy-start(bf16[128,1024]{1,0:T(8,128)(2,1)} %query_ref.1) | copy-start | bytes 786436
  1.0 1.6 %copy-start.3 = (s32[4]{0:T(128)S(1)}, s32[4]{0:T(128)}, u32[]{:S(2)}) copy-start(s32[4]{0:T(128)} %doc_ref.1) | copy-start | bytes 52
  2.3 15.8 %copy-start = (bf16[1024,512]{1,0:T(8,128)(2,1)S(1)}, bf16[1024,512]{1,0:T(8,128)(2,1)}, u32[]{:S(2)}) copy-start(bf16[1024,512]{1,0:T(8,128)(2,1)} %weight_ref.1) | copy-start | bytes 3145732
  2.5 15.6 %copy-start.2 = (bf16[128,1024]{1,0:T(8,128)(2,1)S(1)}, bf16[128,1024]{1,0:T(8,128)(2,1)}, u32[]{:S(2)}) copy-start(bf16[128,1024]{1,0:T(8,128)(2,1)} %gate_ref.1) | copy-start | bytes 786436
  18.1 0.7 %copy-start.4 = (f32[128]{0:T(128)S(1)}, f32[128]{0:T(128)}, u32[]{:S(2)}) copy-start(f32[128]{0:T(128)} %param.16) | copy-start | bytes 1540

commit v3 on v2

v3 whole, which is shorter than its diff:
```python
import jax
import jax.numpy as jnp
from jax import lax
from jax.experimental import pallas as pl
from jax.experimental.pallas import tpu as pltpu
from jax.sharding import PartitionSpec as P

F32 = jnp.float32
BF16 = jnp.bfloat16


def mm(a, b):
    return jnp.dot(a.astype(BF16), b.astype(BF16), preferred_element_type=F32)


def mm_nt(a, b):
    return lax.dot_general(
        a.astype(BF16), b.astype(BF16), (((1,), (1,)), ((), ())), preferred_element_type=F32
    )


def mm_tn(a, b):
    return lax.dot_general(
        a.astype(BF16), b.astype(BF16), (((0,), (0,)), ((), ())), preferred_element_type=F32
    )


def iota(shape, dim):
    return lax.broadcasted_iota(jnp.int32, shape, dim)


def unit_lower_inverse(parts, half):
    rows, cols = iota((half, half), 0), iota((half, half), 1)
    size = 1
    inverses = None
    while size < half:
        row_block, col_block = rows // size, cols // size
        link = (row_block == col_block + 1) & (row_block % 2 == 1)
        linked = [jnp.where(link, part, 0.0) for part in parts]
        if inverses is None:
            eye = jnp.where(rows == cols, 1.0, 0.0)
            inverses = [eye - part for part in linked]
        else:
            short = [inverse.astype(BF16) for inverse in inverses]
            middle = [mm(part, inverse) for part, inverse in zip(linked, short)]
            fixes = [mm(inverse, part) for inverse, part in zip(short, middle)]
            inverses = [inverse - fix for inverse, fix in zip(inverses, fixes)]
        size *= 2
    return inverses


class Frame:
    def __init__(self, doc_ref, tokens, first):
        steps, half = 2 * tokens, tokens
        docs = doc_ref.shape[0]

        def doc_of(position):
            return sum((position >= doc_ref[index]).astype(jnp.int32) for index in range(docs))

        self.tokens, self.steps, self.half = tokens, steps, half
        self.doc_before = doc_of(first - 1)
        self.doc_last = doc_of(first + tokens - 1)
        self.step_doc_col = doc_of(first + iota((steps, half), 0) // 2)
        self.step_doc_row = doc_of(first + iota((1, steps), 1) // 2)
        self.token_doc_col = doc_of(first + iota((tokens, steps), 0))
        col_ids = iota((tokens, steps), 1)
        self.score_mask = (col_ids <= 2 * iota((tokens, steps), 0) + 1) & (
            self.token_doc_col == self.step_doc_row
        )
        self.step_tri = (iota((steps, tokens), 1) <= iota((steps, tokens), 0) // 2).astype(BF16)
        self.token_tri = (iota((tokens, tokens), 1) <= iota((tokens, tokens), 0)).astype(BF16)
        self.row_tri = (iota((tokens, steps), 0) <= iota((tokens, steps), 1) // 2).astype(BF16)
        rows, cols = iota((half, half), 0), iota((half, half), 1)
        self.eye = rows == cols
        lower = rows > cols
        self.docs_low = self.step_doc_col[half:] == self.step_doc_row[:, :half]
        self.docs_first = (self.step_doc_col[:half] == self.step_doc_row[:, :half]) & lower
        self.docs_second = (self.step_doc_col[half:] == self.step_doc_row[:, half:]) & lower
        self.eye_steps = (iota((steps, steps), 0) == iota((steps, steps), 1)).astype(BF16)


def head_lanes(head, depth):
    return pl.ds(pl.multiple_of(head * depth, depth), depth)


def head_decay(frame, decay_ref, head, depth):
    pick = (iota((decay_ref.shape[1], depth), 0) == head).astype(BF16)
    decay_col = mm(decay_ref[...], pick)
    return decay_col, mm_tn(decay_col, frame.row_tri)[:1]


def state_phase(frame, heads, key_ref, value_ref, rate_ref, decay_ref, keep, state_ref, depth):
    half, steps = frame.half, frame.steps
    parts, corners, work = [], [], []
    for head in heads:
        pick = (iota((rate_ref.shape[1], depth), 0) == head).astype(BF16)
        lanes = head_lanes(head, depth)
        key, value = key_ref[:, lanes], value_ref[:, lanes]
        rate_col = mm(rate_ref[...], pick)
        decay_col, total_row = head_decay(frame, decay_ref, head, depth)
        total_col = mm(frame.step_tri, decay_col)
        rate_row = mm_tn(rate_col, frame.eye_steps)[:1]
        key_one, key_two = key[:half], key[half:]
        gram_one, gram_two = mm_nt(key_one, key_one), mm_nt(key_two, key_two)
        gram_low = mm_nt(key_two, key_one)
        diag_one = jnp.where(frame.eye, gram_one, 0.0)
        diag_two = jnp.where(frame.eye, gram_two, 0.0)
        inv_row = lax.rsqrt(
            jnp.concatenate(
                [jnp.sum(diag_one, 0, keepdims=True), jnp.sum(diag_two, 0, keepdims=True)], 1
            )
            + 1e-06
        )
        inv_col = lax.rsqrt(
            jnp.concatenate(
                [jnp.sum(diag_one, 1, keepdims=True), jnp.sum(diag_two, 1, keepdims=True)], 0
            )
            + 1e-06
        )
        left = rate_col * inv_col

        def linked(gram, mask, rows, cols):
            ratio = jnp.exp(jnp.minimum(total_col[rows] - total_row[:, cols], 0.0))
            return jnp.where(mask, gram * left[rows] * inv_row[:, cols] * ratio, 0.0)

        upper, lower = slice(0, half), slice(half, steps)
        parts.append(linked(gram_one, frame.docs_first, upper, upper))
        parts.append(linked(gram_two, frame.docs_second, lower, lower))
        corners.append(linked(gram_low, frame.docs_low, lower, upper))
        work.append((key, value, total_col, total_row, rate_row, inv_row, inv_col))

    inverses = unit_lower_inverse(parts, half)
    for local, head in enumerate(heads):
        key, value, total_col, total_row, rate_row, inv_row, inv_col = work[local]
        inv_one, inv_two = inverses[2 * local], inverses[2 * local + 1]
        inv_low = -mm(inv_two, mm(corners[local], inv_one))
        start_row = jnp.where(
            frame.step_doc_row == frame.doc_before, jnp.exp(total_row), 0.0
        )
        last = total_col[steps - 1 :]
        end_col = inv_col * jnp.where(
            frame.step_doc_col == frame.doc_last, jnp.exp(last - total_col), 0.0
        )

        def solve(scale, right):
            first_rows = mm(inv_one * scale[:, :half], right[:half])
            left = jnp.concatenate([inv_low * scale[:, :half], inv_two * scale[:, half:]], 1)
            return jnp.concatenate([first_rows, mm(left, right)], 0)

        written = solve(rate_row, value)
        erased = solve(rate_row * start_row * inv_row, key)
        last_gain = jnp.where(frame.doc_last == frame.doc_before, jnp.exp(last), 0.0)
        state_ref[head, 0] = (
            jnp.where(frame.eye, last_gain, 0.0) - mm_tn(key, erased * end_col)
        ).astype(BF16)
        state_ref[head, 1] = mm_tn(key, written * end_col).astype(BF16)
        written_ref, erased_ref, inverse_ref = keep
        written_ref[head] = written.astype(BF16)
        erased_ref[head] = erased.astype(BF16)
        inverse_ref[head] = inv_row


def read_phase(frame, head, query_ref, key_ref, decay_ref, keep, inner_ref, carried_ref, depth):
    written_ref, erased_ref, inverse_ref = keep
    lanes = head_lanes(head, depth)
    query, key = query_ref[:, lanes], key_ref[:, lanes]
    decay_col, total_row = head_decay(frame, decay_ref, head, depth)
    token_col = mm(frame.token_tri, decay_col)
    token_wide = jnp.concatenate([token_col, token_col], 1)
    start_token = jnp.where(
        frame.token_doc_col[:, : frame.half] == frame.doc_before, jnp.exp(token_col), 0.0
    )
    ratio = jnp.exp(jnp.minimum(token_wide - total_row, 0.0))
    scores = jnp.where(frame.score_mask, mm_nt(query, key) * inverse_ref[head] * ratio, 0.0)
    scores = scores.astype(BF16)
    inner_ref[:, lanes] = mm(scores, written_ref[head])
    carried_ref[:, lanes] = (
        start_token * query.astype(F32) - mm(scores, erased_ref[head])
    ).astype(carried_ref.dtype)


MESH = pl.DeviceIdType.MESH


def join_kernel(
    doc_ref,
    query_ref,
    key_ref,
    value_ref,
    rate_ref,
    decay_ref,
    gate_ref,
    gain_ref,
    weight_ref,
    out_ref,
    inner_ref,
    carried_ref,
    state_ref,
    written_ref,
    erased_ref,
    inverse_ref,
    mine,
    relay_out,
    relay_in,
    starts,
    back,
    normed,
    deal_send,
    deal_recv,
    relay_send,
    relay_recv,
    back_send,
    back_recv,
    far_send,
    far_recv,
    near_send,
    near_recv,
):
    groups, heads_here, _, depth, _ = mine.shape
    hops = relay_in.shape[0]
    heads_all = groups * heads_here
    tokens = query_ref.shape[0]
    block = heads_here * depth
    me, place, places = lax.axis_index("head"), lax.axis_index("seq"), lax.axis_size("seq")
    has_next, has_prior = place < places - 1, place > 0
    chips = groups // 2
    sibling = me + 1 - 2 * lax.rem(me, 2)

    def to_head(source, target, send, recv, peer):
        return pltpu.make_async_remote_copy(
            src_ref=source,
            dst_ref=target,
            send_sem=send,
            recv_sem=recv,
            device_id={"head": peer},
            device_id_type=MESH,
        )

    barrier = pltpu.get_barrier_semaphore()
    for offset in range(1, groups):
        pl.semaphore_signal(
            barrier, inc=1, device_id={"head": lax.rem(me + offset, groups)}, device_id_type=MESH
        )

    @pl.when(has_next)
    def _():
        pl.semaphore_signal(barrier, inc=1, device_id={"seq": place + 1}, device_id_type=MESH)

    @pl.when(has_prior)
    def _():
        pl.semaphore_signal(barrier, inc=1, device_id={"seq": place - 1}, device_id_type=MESH)

    @pl.when(place == 0)
    def _():
        relay_in[...] = jnp.zeros_like(relay_in)

    frame = Frame(doc_ref, tokens, (place * groups + me) * tokens)
    keep = (written_ref, erased_ref, inverse_ref)
    order = []
    for chip in range(1, chips):
        order += [lax.rem(me + 2 * chip, groups), lax.rem(sibling + 2 * chip, groups)]
    order += [sibling, me]
    together = max(1, 4 // heads_here)
    deals = []
    for begin in range(0, groups, together):
        batch = list(range(begin, min(begin + together, groups)))
        heads = [order[spot] * heads_here + local for spot in batch for local in range(heads_here)]
        state_phase(
            frame, heads, key_ref, value_ref, rate_ref, decay_ref, keep, state_ref, depth
        )
        if begin == 0:
            pl.semaphore_wait(
                barrier, groups - 1 + has_next.astype(jnp.int32) + has_prior.astype(jnp.int32)
            )
        for spot in batch:
            if spot == groups - 1:
                continue
            copy = to_head(
                state_ref.at[pl.ds(order[spot] * heads_here, heads_here)],
                mine.at[me],
                deal_send.at[spot],
                deal_recv.at[spot],
                order[spot],
            )
            copy.start()
            deals.append(copy)
    mine[me] = state_ref[pl.ds(me * heads_here, heads_here)]

    for copy in deals:
        copy.wait_recv()

    sums, maps = [], []
    for local in range(heads_here):
        chain = [None, mine[0, local, 1].astype(F32)]
        for index in range(1, groups):
            chain.append(
                mm(mine[index, local, 0], chain[-1]) + mine[index, local, 1].astype(F32)
            )
        sums.append(chain)

    def relay(hop):
        return pltpu.make_async_remote_copy(
            src_ref=relay_out.at[hop],
            dst_ref=relay_in.at[hop],
            send_sem=relay_send.at[hop],
            recv_sem=relay_recv.at[hop],
            device_id={"seq": place + 1},
            device_id_type=MESH,
        )

    for hop in range(hops):
        for local in range(heads_here):
            value = sums[local][groups]
            if hop:
                value = value + mm(maps[local][groups], relay_in[hop - 1, local])
            relay_out[hop, local] = value.astype(BF16)

        @pl.when(has_next)
        def _(hop=hop):
            relay(hop).start()

        if hop == 0:
            for local in range(heads_here):
                chain = [None, mine[0, local, 0]]
                for index in range(1, groups):
                    chain.append(mm(mine[index, local, 0], chain[-1]).astype(BF16))
                maps.append(chain)

        for head in range(heads_all * hop // hops, heads_all * (hop + 1) // hops):
            read_phase(
                frame, head, query_ref, key_ref, decay_ref, keep, inner_ref, carried_ref, depth
            )

        @pl.when(has_prior)
        def _(hop=hop):
            relay(hop).wait_recv()

    for local in range(heads_here):
        incoming = relay_in[hops - 1, local]
        starts[0, local] = incoming
        for index in range(1, groups):
            starts[index, local] = (
                mm(maps[local][index], incoming) + sums[local][index]
            ).astype(BF16)
    returns = []
    for offset in range(1, groups):
        peer = lax.rem(me + offset, groups)
        copy = to_head(
            starts.at[peer], back.at[me], back_send.at[offset], back_recv.at[offset], peer
        )
        copy.start()
        returns.append(copy)
    back[me] = starts[me]

    gain = gain_ref[...]
    fars, nears = [], []
    for piece in range(groups):
        if piece:
            returns[piece - 1].wait_recv()
        owner = lax.rem(me - piece + groups, groups)
        for local in range(heads_here):
            lanes = pl.ds(pl.multiple_of(owner * block + local * depth, depth), depth)
            readout = inner_ref[:, lanes] + mm(carried_ref[:, lanes], back[owner, local])
            gate = gate_ref[:, lanes].astype(F32)
            inv_rms = lax.rsqrt(jnp.mean(readout * readout, -1, keepdims=True) + 1e-05)
            normed[me, :, lanes] = (
                readout * inv_rms * gain * (gate / (1.0 + jnp.exp(-gate)))
            ).astype(BF16)
        lanes = pl.ds(pl.multiple_of(owner * block, block), block)
        here = normed.at[me, :, lanes]
        for chip in range(1, chips):
            copy = to_head(
                here,
                here,
                far_send.at[piece, chip],
                far_recv.at[piece, chip],
                lax.rem(me + 2 * chip, groups),
            )
            copy.start()
            fars.append((chip, piece, copy))
        copy = to_head(here, here, near_send.at[piece, 0], near_recv.at[piece, 0], sibling)
        copy.start()
        nears.append(copy)

    def project(source):
        rows = pl.ds(pl.multiple_of(source * tokens, tokens), tokens)
        out_ref[rows, :] = jnp.dot(
            normed[source], weight_ref[...], preferred_element_type=F32
        ).astype(out_ref.dtype)

    project(me)
    forwards = []
    for chip, piece, copy in fars:
        source = lax.rem(me - 2 * chip + groups, groups)
        owner = lax.rem(source - piece + groups, groups)
        there = normed.at[source, :, pl.ds(pl.multiple_of(owner * block, block), block)]
        copy.wait_recv()
        onward = to_head(
            there, there, near_send.at[piece, chip], near_recv.at[piece, chip], sibling
        )
        onward.start()
        forwards.append(onward)
    for copy in nears:
        copy.wait_recv()
    project(sibling)
    for chip in range(1, chips):
        project(lax.rem(me - 2 * chip + groups, groups))
    for onward in forwards:
        onward.wait_recv()
    for chip in range(1, chips):
        project(lax.rem(sibling - 2 * chip + groups, groups))

    for copy in deals + returns + [far[2] for far in fars] + nears + forwards:
        copy.wait_send()
    for hop in range(hops):

        @pl.when(has_next)
        def _(hop=hop):
            relay(hop).wait_send()


def on_device(
    queries, keys, values, out_gate, write_rate, log_decay, doc_starts, norm_gain, out_weight
):
    tokens, width = queries.shape
    heads_all = log_decay.shape[1]
    depth = width // heads_all
    groups = lax.axis_size("head")
    heads_here = heads_all // groups
    hops = lax.axis_size("seq") // 2
    steps = 2 * tokens
    sems = pltpu.SemaphoreType.DMA
    return pl.pallas_call(
        join_kernel,
        in_specs=[pl.BlockSpec(memory_space=pltpu.SMEM)]
        + [pl.BlockSpec(memory_space=pltpu.VMEM)] * 8,
        out_specs=pl.BlockSpec(memory_space=pltpu.VMEM),
        out_shape=jax.ShapeDtypeStruct((groups * tokens, out_weight.shape[1]), BF16),
        scratch_shapes=[
            pltpu.VMEM((tokens, width), F32),
            pltpu.VMEM((tokens, width), BF16),
            pltpu.VMEM((heads_all, 2, depth, depth), BF16),
            pltpu.VMEM((heads_all, steps, depth), BF16),
            pltpu.VMEM((heads_all, steps, depth), BF16),
            pltpu.VMEM((heads_all, 1, steps), F32),
            pltpu.VMEM((groups, heads_here, 2, depth, depth), BF16),
            pltpu.VMEM((hops, heads_here, depth, depth), BF16),
            pltpu.VMEM((hops, heads_here, depth, depth), BF16),
            pltpu.VMEM((groups, heads_here, depth, depth), BF16),
            pltpu.VMEM((groups, heads_here, depth, depth), BF16),
            pltpu.VMEM((groups, tokens, width), BF16),
            sems((groups,)),
            sems((groups,)),
            sems((hops,)),
            sems((hops,)),
            sems((groups,)),
            sems((groups,)),
            sems((groups, groups // 2)),
            sems((groups, groups // 2)),
            sems((groups, groups // 2)),
            sems((groups, groups // 2)),
        ],
        compiler_params=pltpu.CompilerParams(
            collective_id=0, has_side_effects=True, vmem_limit_bytes=40 * 1024 * 1024
        ),
        name="join",
    )(
        doc_starts,
        queries,
        keys.reshape(steps, width),
        values.reshape(steps, width),
        write_rate.reshape(steps, heads_all),
        log_decay,
        out_gate,
        norm_gain.reshape(1, depth),
        out_weight,
    )


def solution(mesh):
    placed = (
        P(("rep", "seq", "head"), None),
        P(("rep", "seq", "head"), None, None),
        P(("rep", "seq", "head"), None, None),
        P(("rep", "seq", "head"), None),
        P(("rep", "seq", "head"), None, None),
        P(("rep", "seq", "head"), None),
        P("rep"),
        P(),
        P(None, "head"),
    )
    return jax.shard_map(
        on_device, mesh=mesh, in_specs=placed, out_specs=P(("rep", "seq"), "head"), check_vma=False
    )
```

time: 46.1 us -> 35.6 us (0.77)
  Pallas kernels: 41.7 us -> 31.2 us
    pallas_call x2 -> x1, Pallas kernels: 41.7 us -> 31.2 us  [on_device(): pl.pallas_call(join_kernel, in_specs=[pl.BlockSpec(memory_space=pltpu.SME...]
where the time goes in v3:
time: 35.6 us; the launch traced here: 35.4 us
  Pallas kernels  31.2 us (88%)
  local copies, waits for them, and re-layouts  4.08 us (11%)
    pallas_call x1, Pallas kernels, on_device(): pl.pallas_call(join_kernel, in_specs=[pl.BlockSpec(memory_space=pltpu.SME...  31.2 us
    unnamed x17, local copies, waits for them, and re-layouts  2.55 us
    reshape x1, local copies, waits for them, and re-layouts, on_device(): keys.reshape(steps, width)  1.33 us

profile of v3, /device:TPU:25, one launch (start us, length us, event | category | flops | bytes accessed | tf_op | source)
XLA Modules:
  0.0 35.4 jit_solution(11594028201744848902)
XLA Ops:
  0.0 0.0 copy-start.6
  0.0 0.8 %copy.11.decay_ref = bf16[128,8]{1,0:T(8,128)(2,1)S(1)} copy(bf16[128,8]{0,1:T(8,128)(2,1)} %param.14) | data formatting | bytes 4096 | tf_op args[5]
  0.8 0.0 copy-done.6
  0.8 0.0 copy-start.5
  0.8 0.1 copy.10
  1.0 0.0 copy-start
  1.0 1.3 %reshape.12.key_ref = bf16[256,1024]{1,0:T(8,128)(2,1)S(1)} reshape(bf16[128,2,1024]{2,1,0:T(2,128)(2,1)} %param.10) | data formatting | bytes 1048576 | tf_op jit(solution)/shard_map/reshape | solution.py:470
  2.3 0.0 copy-done.5
  2.3 0.0 copy-start.1
  2.3 0.0 copy-start.2
  2.3 0.0 copy-start.3
  2.4 0.0 copy-start.4
  2.4 0.2 reshape.13.value_ref
  2.6 0.0 copy-done
  2.6 0.7 %copy-done.1 = bf16[128,1024]{1,0:T(8,128)(2,1)S(1)} copy-done((bf16[128,1024]{1,0:T(8,128)(2,1)S(1)}, bf16[128,1024]{1,0:T(8,128)(2,1)}, u32[]{:S(2)}) %copy-start.1) | copy-done | bytes 262168
  3.3 0.1 copy-done.2
  3.4 0.0 copy-done.3
  3.4 0.0 copy-done.4
  3.4 31.2 %join.1 = bf16[512,512]{1,0:T(8,128)(2,1)S(1)} custom-call(s32[4]{0:T(128)S(1)} %copy-done.3, bf16[128,1024]{1,0:T(8,128)(2,1)S(1)} %copy-done.1, bf16[256,1024]{1,0:T(8,128)(2,1)S(1)} %reshape.12.key_ref, bf16[256,1024]{1,0:T(8,128)(2,1)S(1)} %reshape.13.value_ref, bf16[256,8]{1,0:T(8,128)(2,1)S(1)} %bitcast.2, bf16[128,8]{1,0:T(8,128)(2,1)S(1)} %copy.11.decay_ref, ...), custom_call_target="tpu_custom_call" | custom-call | tf_op jit(solution)/shard_map/join/pallas_call | solution.py:433
  34.6 0.8 %copy.13 = bf16[512,512]{1,0:T(8,128)(2,1)} copy(bf16[512,512]{1,0:T(8,128)(2,1)S(1)} %join.1) | data formatting | bytes 1048576
Async XLA Ops:
  0.0 0.8 %copy-start.6 = (bf16[128,2,8]{0,2,1:T(8,128)(2,1)S(1)}, bf16[128,2,8]{0,2,1:T(8,128)(2,1)}, u32[]{:S(2)}) copy-start(bf16[128,2,8]{0,2,1:T(8,128)(2,1)} %param.13) | copy-start | bytes 12292
  0.8 1.5 %copy-start.5 = (bf16[128,2,1024]{2,1,0:T(2,128)(2,1)S(1)}, bf16[128,2,1024]{2,1,0:T(2,128)(2,1)}, u32[]{:S(2)}) copy-start(bf16[128,2,1024]{2,1,0:T(2,128)(2,1)} %param.11) | copy-start | bytes 1572868
  1.0 1.6 %copy-start = (bf16[1024,512]{1,0:T(8,128)(2,1)S(1)}, bf16[1024,512]{1,0:T(8,128)(2,1)}, u32[]{:S(2)}) copy-start(bf16[1024,512]{1,0:T(8,128)(2,1)} %weight_ref.1) | copy-start | bytes 3145732
  2.3 1.0 %copy-start.1 = (bf16[128,1024]{1,0:T(8,128)(2,1)S(1)}, bf16[128,1024]{1,0:T(8,128)(2,1)}, u32[]{:S(2)}) copy-start(bf16[128,1024]{1,0:T(8,128)(2,1)} %query_ref.1) | copy-start | bytes 786436
  2.3 1.0 %copy-start.2 = (bf16[128,1024]{1,0:T(8,128)(2,1)S(1)}, bf16[128,1024]{1,0:T(8,128)(2,1)}, u32[]{:S(2)}) copy-start(bf16[128,1024]{1,0:T(8,128)(2,1)} %gate_ref.1) | copy-start | bytes 786436
  2.3 1.0 %copy-start.3 = (s32[4]{0:T(128)S(1)}, s32[4]{0:T(128)}, u32[]{:S(2)}) copy-start(s32[4]{0:T(128)} %doc_ref.1) | copy-start | bytes 52
  2.4 1.0 %copy-start.4 = (f32[128]{0:T(128)S(1)}, f32[128]{0:T(128)}, u32[]{:S(2)}) copy-start(f32[128]{0:T(128)} %param.16) | copy-start | bytes 1540

commit v4 on v3

--- a/solution.py
+++ b/solution.py
@@ -76,6 +76,8 @@
         self.docs_low = self.step_doc_col[half:] == self.step_doc_row[:, :half]
         self.docs_first = (self.step_doc_col[:half] == self.step_doc_row[:, :half]) & lower
         self.docs_second = (self.step_doc_col[half:] == self.step_doc_row[:, half:]) & lower
+        woven, split = iota((steps, steps), 0), iota((steps, steps), 1)
+        self.weave = (woven == 2 * (split % tokens) + split // tokens).astype(BF16)
         self.eye_steps = (iota((steps, steps), 0) == iota((steps, steps), 1)).astype(BF16)
 
 
@@ -84,8 +86,8 @@
 
 
 def head_decay(frame, decay_ref, head, depth):
-    pick = (iota((decay_ref.shape[1], depth), 0) == head).astype(BF16)
-    decay_col = mm(decay_ref[...], pick)
+    pick = (iota((decay_ref.shape[0], depth), 0) == head).astype(BF16)
+    decay_col = mm_tn(decay_ref[...], pick)
     return decay_col, mm_tn(decay_col, frame.row_tri)[:1]
 
 
@@ -93,10 +95,11 @@
     half, steps = frame.half, frame.steps
     parts, corners, work = [], [], []
     for head in heads:
-        pick = (iota((rate_ref.shape[1], depth), 0) == head).astype(BF16)
+        pick = (iota((decay_ref.shape[0], depth), 0) == head).astype(BF16)
         lanes = head_lanes(head, depth)
         key, value = key_ref[:, lanes], value_ref[:, lanes]
-        rate_col = mm(rate_ref[...], pick)
+        rate_split = jnp.concatenate([mm_tn(rate_ref[0], pick), mm_tn(rate_ref[1], pick)], 0)
+        rate_col = mm(frame.weave, rate_split)
         decay_col, total_row = head_decay(frame, decay_ref, head, depth)
         total_col = mm(frame.step_tri, decay_col)
         rate_row = mm_tn(rate_col, frame.eye_steps)[:1]
@@ -189,10 +192,13 @@
     value_ref,
     rate_ref,
     decay_ref,
+    gate_hbm,
+    gain_ref,
+    weight_hbm,
+    out_ref,
     gate_ref,
-    gain_ref,
     weight_ref,
-    out_ref,
+    load_sems,
     inner_ref,
     carried_ref,
     state_ref,
@@ -236,6 +242,10 @@
             device_id_type=MESH,
         )
 
+    weight_load = pltpu.make_async_copy(weight_hbm, weight_ref, load_sems.at[0])
+    gate_load = pltpu.make_async_copy(gate_hbm, gate_ref, load_sems.at[1])
+    weight_load.start()
+    gate_load.start()
     barrier = pltpu.get_barrier_semaphore()
     for offset in range(1, groups):
         pl.semaphore_signal(
@@ -343,21 +353,30 @@
                 mm(maps[local][index], incoming) + sums[local][index]
             ).astype(BF16)
     returns = []
-    for offset in range(1, groups):
-        peer = lax.rem(me + offset, groups)
+    for spot in range(groups - 1):
         copy = to_head(
-            starts.at[peer], back.at[me], back_send.at[offset], back_recv.at[offset], peer
+            starts.at[order[spot]], back.at[me], back_send.at[spot], back_recv.at[spot], order[spot]
         )
         copy.start()
         returns.append(copy)
     back[me] = starts[me]
 
+    gate_load.wait()
     gain = gain_ref[...]
     fars, nears = [], []
+    spots = [groups - 1, groups - 2, *range(groups - 2)]
+
+    def owner_of(device, piece):
+        spot = spots[piece]
+        other = device + 1 - 2 * lax.rem(device, 2)
+        base = other if spot == groups - 2 or (spot < groups - 2 and spot % 2) else device
+        shift = 0 if spot >= groups - 2 else 2 * (spot // 2 + 1)
+        return lax.rem(base - shift + groups, groups)
+
     for piece in range(groups):
         if piece:
-            returns[piece - 1].wait_recv()
-        owner = lax.rem(me - piece + groups, groups)
+            returns[spots[piece]].wait_recv()
+        owner = owner_of(me, piece)
         for local in range(heads_here):
             lanes = pl.ds(pl.multiple_of(owner * block + local * depth, depth), depth)
             readout = inner_ref[:, lanes] + mm(carried_ref[:, lanes], back[owner, local])
@@ -388,11 +407,12 @@
             normed[source], weight_ref[...], preferred_element_type=F32
         ).astype(out_ref.dtype)
 
+    weight_load.wait()
     project(me)
     forwards = []
     for chip, piece, copy in fars:
         source = lax.rem(me - 2 * chip + groups, groups)
-        owner = lax.rem(source - piece + groups, groups)
+        owner = owner_of(source, piece)
         there = normed.at[source, :, pl.ds(pl.multiple_of(owner * block, block), block)]
         copy.wait_recv()
         onward = to_head(
@@ -433,10 +453,18 @@
     return pl.pallas_call(
         join_kernel,
         in_specs=[pl.BlockSpec(memory_space=pltpu.SMEM)]
-        + [pl.BlockSpec(memory_space=pltpu.VMEM)] * 8,
+        + [pl.BlockSpec(memory_space=pltpu.VMEM)] * 5
+        + [
+            pl.BlockSpec(memory_space=pltpu.HBM),
+            pl.BlockSpec(memory_space=pltpu.VMEM),
+            pl.BlockSpec(memory_space=pltpu.HBM),
+        ],
         out_specs=pl.BlockSpec(memory_space=pltpu.VMEM),
         out_shape=jax.ShapeDtypeStruct((groups * tokens, out_weight.shape[1]), BF16),
         scratch_shapes=[
+            pltpu.VMEM(out_gate.shape, BF16),
+            pltpu.VMEM(out_weight.shape, BF16),
+            sems((2,)),
             pltpu.VMEM((tokens, width), F32),
             pltpu.VMEM((tokens, width), BF16),
             pltpu.VMEM((heads_all, 2, depth, depth), BF16),
@@ -469,8 +497,8 @@
         queries,
         keys.reshape(steps, width),
         values.reshape(steps, width),
-        write_rate.reshape(steps, heads_all),
-        log_decay,
+        write_rate.transpose(1, 2, 0),
+        log_decay.T,
         out_gate,
         norm_gain.reshape(1, depth),
         out_weight,

time: 35.6 us -> 36.3 us (1.020)
  Pallas kernels: 31.2 us -> 32.6 us
  local copies, waits for them, and re-layouts: 4.08 us -> 3.45 us
    unnamed x17 -> x15, local copies, waits for them, and re-layouts: 2.55 us -> 0.84 us
    pallas_call x1, Pallas kernels: 31.2 us -> 32.6 us  [on_device(): pl.pallas_call(join_kernel, in_specs=[pl.BlockSpec(memory_space=pltpu.SME...]
    reshape x1, local copies, waits for them, and re-layouts: 0.2 us -> 1.29 us  [on_device(): values.reshape(steps, width)]
where the time goes in v4:
time: 36.3 us; the launch traced here: 36.2 us
  Pallas kernels  32.6 us (90%)
  local copies, waits for them, and re-layouts  3.45 us (10%)
    pallas_call x1, Pallas kernels, on_device(): pl.pallas_call(join_kernel, in_specs=[pl.BlockSpec(memory_space=pltpu.SME...  32.6 us
    reshape x1, local copies, waits for them, and re-layouts, on_device(): keys.reshape(steps, width)  1.33 us
    reshape x1, local copies, waits for them, and re-layouts, on_device(): values.reshape(steps, width)  1.29 us
    unnamed x15, local copies, waits for them, and re-layouts  0.84 us

profile of v4, /device:TPU:25, one launch (start us, length us, event | category | flops | bytes accessed | tf_op | source)
XLA Modules:
  0.0 36.2 jit_solution(9876402377792623497)
XLA Ops:
  0.0 0.0 copy-start
  0.0 1.3 %reshape.9.key_ref = bf16[256,1024]{1,0:T(8,128)(2,1)S(1)} reshape(bf16[128,2,1024]{2,1,0:T(2,128)(2,1)} %param.10) | data formatting | bytes 1048576 | tf_op jit(solution)/shard_map/reshape | solution.py:498
  1.3 0.0 copy-start.1
  1.3 0.0 copy-start.2
  1.4 0.0 copy-start.3
  1.4 0.0 copy-start.4
  1.4 0.0 copy-start.5
  1.4 0.0 copy-start.6
  1.4 1.3 %reshape.10.value_ref = bf16[256,1024]{1,0:T(8,128)(2,1)S(1)} reshape(bf16[128,2,1024]{2,1,0:T(2,128)(2,1)} %param.11) | data formatting | bytes 1048576 | tf_op jit(solution)/shard_map/reshape | solution.py:499
  2.7 0.0 copy-done
  2.7 0.0 copy-done.1
  2.7 0.0 copy-done.2
  2.7 0.0 copy-done.3
  2.7 0.0 copy-done.4
  2.7 0.0 copy-done.5
  2.8 0.0 copy-done.6
  2.8 32.6 %join.1 = bf16[512,512]{1,0:T(8,128)(2,1)S(1)} custom-call(s32[4]{0:T(128)S(1)} %copy-done.5, bf16[128,1024]{1,0:T(8,128)(2,1)S(1)} %copy-done.1, bf16[256,1024]{1,0:T(8,128)(2,1)S(1)} %reshape.9.key_ref, bf16[256,1024]{1,0:T(8,128)(2,1)S(1)} %reshape.10.value_ref, bf16[2,8,128]{2,1,0:T(8,128)(2,1)S(1)} %bitcast.3, bf16[8,128]{1,0:T(8,128)(2,1)S(1)} %bitcast.4, ...), custom_call_target="tpu_custom_call" | custom-call | tf_op jit(solution)/shard_map/join/pallas_call | solution.py:453
  35.4 0.8 %copy.11 = bf16[512,512]{1,0:T(8,128)(2,1)} copy(bf16[512,512]{1,0:T(8,128)(2,1)S(1)} %join.1) | data formatting | bytes 1048576
Async XLA Ops:
  0.0 2.7 %copy-start = (bf16[1024,512]{1,0:T(8,128)(2,1)S(1)}, bf16[1024,512]{1,0:T(8,128)(2,1)}, u32[]{:S(2)}) copy-start(bf16[1024,512]{1,0:T(8,128)(2,1)} %weight_hbm.1) | copy-start | bytes 3145732
  1.3 1.4 %copy-start.1 = (bf16[128,1024]{1,0:T(8,128)(2,1)S(1)}, bf16[128,1024]{1,0:T(8,128)(2,1)}, u32[]{:S(2)}) copy-start(bf16[128,1024]{1,0:T(8,128)(2,1)} %query_ref.1) | copy-start | bytes 786436
  1.3 1.4 %copy-start.2 = (bf16[128,1024]{1,0:T(8,128)(2,1)S(1)}, bf16[128,1024]{1,0:T(8,128)(2,1)}, u32[]{:S(2)}) copy-start(bf16[128,1024]{1,0:T(8,128)(2,1)} %gate_hbm.1) | copy-start | bytes 786436
  1.4 1.4 %copy-start.3 = (bf16[128,2,8]{0,2,1:T(8,128)(2,1)S(1)}, bf16[128,2,8]{0,2,1:T(8,128)(2,1)}, u32[]{:S(2)}) copy-start(bf16[128,2,8]{0,2,1:T(8,128)(2,1)} %param.13) | copy-start | bytes 12292
  1.4 1.4 %copy-start.4 = (bf16[128,8]{0,1:T(8,128)(2,1)S(1)}, bf16[128,8]{0,1:T(8,128)(2,1)}, u32[]{:S(2)}) copy-start(bf16[128,8]{0,1:T(8,128)(2,1)} %param.14) | copy-start | bytes 6148
  1.4 1.4 %copy-start.5 = (s32[4]{0:T(128)S(1)}, s32[4]{0:T(128)}, u32[]{:S(2)}) copy-start(s32[4]{0:T(128)} %doc_ref.1) | copy-start | bytes 52
  1.4 1.4 %copy-start.6 = (f32[128]{0:T(128)S(1)}, f32[128]{0:T(128)}, u32[]{:S(2)}) copy-start(f32[128]{0:T(128)} %param.16) | copy-start | bytes 1540

commit v5 on v3

--- a/solution.py
+++ b/solution.py
@@ -343,10 +343,9 @@
                 mm(maps[local][index], incoming) + sums[local][index]
             ).astype(BF16)
     returns = []
-    for offset in range(1, groups):
-        peer = lax.rem(me + offset, groups)
+    for spot in range(groups - 1):
         copy = to_head(
-            starts.at[peer], back.at[me], back_send.at[offset], back_recv.at[offset], peer
+            starts.at[order[spot]], back.at[me], back_send.at[spot], back_recv.at[spot], order[spot]
         )
         copy.start()
         returns.append(copy)
@@ -354,10 +353,19 @@
 
     gain = gain_ref[...]
     fars, nears = [], []
+    spots = [groups - 1, groups - 2, *range(groups - 2)]
+
+    def owner_of(device, piece):
+        spot = spots[piece]
+        other = device + 1 - 2 * lax.rem(device, 2)
+        base = other if spot == groups - 2 or (spot < groups - 2 and spot % 2) else device
+        shift = 0 if spot >= groups - 2 else 2 * (spot // 2 + 1)
+        return lax.rem(base - shift + groups, groups)
+
     for piece in range(groups):
         if piece:
-            returns[piece - 1].wait_recv()
-        owner = lax.rem(me - piece + groups, groups)
+            returns[spots[piece]].wait_recv()
+        owner = owner_of(me, piece)
         for local in range(heads_here):
             lanes = pl.ds(pl.multiple_of(owner * block + local * depth, depth), depth)
             readout = inner_ref[:, lanes] + mm(carried_ref[:, lanes], back[owner, local])
@@ -392,7 +400,7 @@
     forwards = []
     for chip, piece, copy in fars:
         source = lax.rem(me - 2 * chip + groups, groups)
-        owner = lax.rem(source - piece + groups, groups)
+        owner = owner_of(source, piece)
         there = normed.at[source, :, pl.ds(pl.multiple_of(owner * block, block), block)]
         copy.wait_recv()
         onward = to_head(

time: 35.6 us -> 35.6 us (level)
  no operation moved by 1% of the time
where the time goes in v5:
time: 35.6 us; the launch traced here: 35.4 us
  Pallas kernels  31.2 us (88%)
  local copies, waits for them, and re-layouts  4.08 us (11%)
    pallas_call x1, Pallas kernels, on_device(): pl.pallas_call(join_kernel, in_specs=[pl.BlockSpec(memory_space=pltpu.SME...  31.2 us
    unnamed x17, local copies, waits for them, and re-layouts  2.55 us
    reshape x1, local copies, waits for them, and re-layouts, on_device(): keys.reshape(steps, width)  1.33 us

profile of v5, /device:TPU:25, one launch (start us, length us, event | category | flops | bytes accessed | tf_op | source)
XLA Modules:
  0.0 35.4 jit_solution(9006831332098614524)
XLA Ops:
  0.0 0.0 copy-start.6
  0.0 0.8 %copy.11.decay_ref = bf16[128,8]{1,0:T(8,128)(2,1)S(1)} copy(bf16[128,8]{0,1:T(8,128)(2,1)} %param.14) | data formatting | bytes 4096 | tf_op args[5]
  0.8 0.0 copy-done.6
  0.8 0.0 copy-start.5
  0.8 0.1 copy.10
  1.0 0.0 copy-start
  1.0 1.3 %reshape.12.key_ref = bf16[256,1024]{1,0:T(8,128)(2,1)S(1)} reshape(bf16[128,2,1024]{2,1,0:T(2,128)(2,1)} %param.10) | data formatting | bytes 1048576 | tf_op jit(solution)/shard_map/reshape | solution.py:478
  2.3 0.0 copy-done.5
  2.3 0.0 copy-start.1
  2.3 0.0 copy-start.2
  2.3 0.0 copy-start.3
  2.4 0.0 copy-start.4
  2.4 0.2 reshape.13.value_ref
  2.6 0.0 copy-done
  2.6 0.7 %copy-done.1 = bf16[128,1024]{1,0:T(8,128)(2,1)S(1)} copy-done((bf16[128,1024]{1,0:T(8,128)(2,1)S(1)}, bf16[128,1024]{1,0:T(8,128)(2,1)}, u32[]{:S(2)}) %copy-start.1) | copy-done | bytes 262168
  3.3 0.1 copy-done.2
  3.4 0.0 copy-done.3
  3.4 0.0 copy-done.4
  3.4 31.2 %join.1 = bf16[512,512]{1,0:T(8,128)(2,1)S(1)} custom-call(s32[4]{0:T(128)S(1)} %copy-done.3, bf16[128,1024]{1,0:T(8,128)(2,1)S(1)} %copy-done.1, bf16[256,1024]{1,0:T(8,128)(2,1)S(1)} %reshape.12.key_ref, bf16[256,1024]{1,0:T(8,128)(2,1)S(1)} %reshape.13.value_ref, bf16[256,8]{1,0:T(8,128)(2,1)S(1)} %bitcast.2, bf16[128,8]{1,0:T(8,128)(2,1)S(1)} %copy.11.decay_ref, ...), custom_call_target="tpu_custom_call" | custom-call | tf_op jit(solution)/shard_map/join/pallas_call | solution.py:441
  34.6 0.8 %copy.13 = bf16[512,512]{1,0:T(8,128)(2,1)} copy(bf16[512,512]{1,0:T(8,128)(2,1)S(1)} %join.1) | data formatting | bytes 1048576
Async XLA Ops:
  0.0 0.8 %copy-start.6 = (bf16[128,2,8]{0,2,1:T(8,128)(2,1)S(1)}, bf16[128,2,8]{0,2,1:T(8,128)(2,1)}, u32[]{:S(2)}) copy-start(bf16[128,2,8]{0,2,1:T(8,128)(2,1)} %param.13) | copy-start | bytes 12292
  0.8 1.5 %copy-start.5 = (bf16[128,2,1024]{2,1,0:T(2,128)(2,1)S(1)}, bf16[128,2,1024]{2,1,0:T(2,128)(2,1)}, u32[]{:S(2)}) copy-start(bf16[128,2,1024]{2,1,0:T(2,128)(2,1)} %param.11) | copy-start | bytes 1572868
  1.0 1.6 %copy-start = (bf16[1024,512]{1,0:T(8,128)(2,1)S(1)}, bf16[1024,512]{1,0:T(8,128)(2,1)}, u32[]{:S(2)}) copy-start(bf16[1024,512]{1,0:T(8,128)(2,1)} %weight_ref.1) | copy-start | bytes 3145732
  2.3 1.0 %copy-start.1 = (bf16[128,1024]{1,0:T(8,128)(2,1)S(1)}, bf16[128,1024]{1,0:T(8,128)(2,1)}, u32[]{:S(2)}) copy-start(bf16[128,1024]{1,0:T(8,128)(2,1)} %query_ref.1) | copy-start | bytes 786436
  2.3 1.0 %copy-start.2 = (bf16[128,1024]{1,0:T(8,128)(2,1)S(1)}, bf16[128,1024]{1,0:T(8,128)(2,1)}, u32[]{:S(2)}) copy-start(bf16[128,1024]{1,0:T(8,128)(2,1)} %gate_ref.1) | copy-start | bytes 786436
  2.3 1.0 %copy-start.3 = (s32[4]{0:T(128)S(1)}, s32[4]{0:T(128)}, u32[]{:S(2)}) copy-start(s32[4]{0:T(128)} %doc_ref.1) | copy-start | bytes 52
  2.4 1.0 %copy-start.4 = (f32[128]{0:T(128)S(1)}, f32[128]{0:T(128)}, u32[]{:S(2)}) copy-start(f32[128]{0:T(128)} %param.16) | copy-start | bytes 1540
